TPU v7x, 512 devices: a whole 4x8x8 slice. The times are simulated.
512 devices in a mesh: dp: 32 (over x, y), seq: 16 (over z, core).
Axes of the slice: x: 4, y: 8, z: 8, core: 2. Of those that a mesh axis runs over, the one named last changes fastest.
Arguments:
- projected: bfloat16 [163840, 6144], P(('dp', 'seq')), parts along dimension 0, may hold values from -16 to 16, as said below
- kept_index: int32 [81920], P('dp'), parts along dimension 0, may hold values from 0 to 5119, as said below
Outputs:
- attended: bfloat16 [81920, 2048], P(('dp', 'seq')), parts along dimension 0
There are 32 independent parts, one for each index of `dp`. A program takes and returns all parts, laid end to end along the dimension named above; each array names one. Nothing has to cross between parts.
Inputs may be any that keep to these rules, and one draw needn't show every extreme that they name: `kept_index`: strictly ascending. With P(t) the number of entries below t * 320, P(t) - t * 160 lies within -80 to 80 for every tile t, and both ends are reached in every draw; a tile may keep from none to all of its tokens. `projected`: real values.
All inputs are finite; a program needn't handle non-finite values.
Results may differ from a plain program's by a relative error of at most 0.0048.
Values may be sent and summed in bfloat16 or wider, within the bound.
No kernel may reach another device: no remote copies, remote signals or barrier semaphores. Data moves between devices by JAX's collectives and lax.ppermute only.
A program may use at most 64 MiB of HBM per device.

v0:
```python
import jax
import jax.numpy as jnp
from jax import lax
from jax.sharding import PartitionSpec as P

H = 16
HD = 128


def passed_along(block, axis, distance):
    devices = range(lax.axis_size(axis))
    route = [(i - distance, i) for i in devices if i - distance in devices]
    return lax.ppermute(block, axis, route)


def attend_heads(triples):
    total = triples.shape[0]
    count = triples.shape[2]
    hsize = triples.shape[3]
    queries = triples[:, 0]
    key_rows = triples[:, 1]
    value_rows = triples[:, 2]
    block_rows = 512
    blocks = total // block_rows

    def one_block(query_block):
        scores = jnp.einsum(
            "qhd,khd->hqk", query_block, key_rows, preferred_element_type=jnp.float32
        ) * hsize ** (-0.5)
        row_max = jnp.max(scores, axis=-1, keepdims=True)
        weights = jnp.exp(scores - row_max)
        totals = jnp.sum(weights, axis=-1)
        mixed = jnp.einsum(
            "hqk,khd->qhd",
            weights.astype(jnp.bfloat16),
            value_rows,
            preferred_element_type=jnp.float32,
        )
        return (mixed / jnp.transpose(totals)[:, :, None]).astype(jnp.bfloat16)

    outputs = lax.map(one_block, queries.reshape(blocks, block_rows, count, hsize))
    return outputs.reshape(total, count, hsize)


def flatten_group(grouped):
    return grouped.reshape(grouped.shape[0], 3, grouped.shape[3], grouped.shape[4])


def local(projected, kept_index):
    device_count = lax.axis_size("seq")
    device_place = lax.axis_index("seq")
    tile_rows = projected.shape[0]
    kept_total = kept_index.shape[0]
    shard_rows = kept_total // device_count
    spill_rows = tile_rows // 4
    local_heads = H // device_count
    first_token = device_place * tile_rows
    begin_place = jnp.sum((kept_index < first_token).astype(jnp.int32))
    end_place = jnp.sum((kept_index < first_token + tile_rows).astype(jnp.int32))

    def select_rows(places, usable):
        bounded = jnp.clip(places, 0, kept_total - 1)
        within = jnp.clip(kept_index[bounded] - first_token, 0, tile_rows - 1)
        picked = jnp.take(projected, within, axis=0)
        return jnp.where(usable[:, None], picked, jnp.zeros_like(picked))

    shard_begin = device_place * shard_rows
    offsets = jnp.arange(spill_rows, dtype=jnp.int32)
    right_place = shard_begin + shard_rows + offsets
    right_rows = select_rows(right_place, right_place < end_place)
    left_place = shard_begin - spill_rows + offsets
    left_rows = select_rows(left_place, left_place >= begin_place)
    from_left = passed_along(right_rows, "seq", 1)
    from_right = passed_along(left_rows, "seq", -1)
    own_place = shard_begin + jnp.arange(shard_rows, dtype=jnp.int32)
    own_rows = select_rows(own_place, (own_place >= begin_place) & (own_place < end_place))
    filler = jnp.zeros((shard_rows - spill_rows, own_rows.shape[1]), own_rows.dtype)
    lower = jnp.concatenate([from_left, filler], axis=0)
    upper = jnp.concatenate([filler, from_right], axis=0)
    shard_data = jnp.where(
        (own_place < begin_place)[:, None],
        lower,
        jnp.where((own_place >= end_place)[:, None], upper, own_rows),
    )
    grouped = shard_data.reshape(shard_rows, 3, device_count, local_heads, HD)
    attended = attend_heads(
        flatten_group(lax.all_to_all(grouped, "seq", split_axis=2, concat_axis=0, tiled=True))
    )
    returned = lax.all_to_all(attended, "seq", split_axis=0, concat_axis=1, tiled=True)
    return returned.reshape(shard_rows, H * HD)


def solution(mesh):
    return jax.shard_map(
        local,
        mesh=mesh,
        in_specs=(P(("dp", "seq"), None), P("dp")),
        out_specs=P(("dp", "seq"), None),
        check_vma=False,
    )
```

profile of v0, /device:TPU:1, one launch (start us, length us, event | category | flops | bytes accessed | tf_op | source)
XLA Modules:
  0.0 142.1 jit_solution(16854112255808217760)
XLA Ops:
  0.1 1.6 %gather_fusion = s32[80]{0:T(128)S(1)} fusion(s32[2560]{0:T(1024)} %param.7, s32[1024]{0:T(1024)S(1)} %pad_clamp_fusion.5), kind=kCustom, calls=%fused_computation.2 | custom fusion | bytes 960 | tf_op jit(solution)/shard_map/gather | solution.py:63
  1.7 1.6 %gather_fusion.1 = s32[80]{0:T(128)S(1)} fusion(s32[2560]{0:T(1024)} %param.7, s32[1024]{0:T(1024)S(1)} %pad_clamp_fusion.3), kind=kCustom, calls=%fused_computation.3 | custom fusion | bytes 960 | tf_op jit(solution)/shard_map/gather | solution.py:63
  3.4 1.4 convert_reduce_fusion
  5.3 4.7 %gather_fusion.5 = bf16[80,6144]{1,0:T(8,128)(2,1)S(1)} fusion(bf16[320,6144]{1,0:T(8,128)(2,1)} %param.6, s32[1024]{0:T(1024)S(1)} %pad_clamp_fusion.2), kind=kCustom, calls=%fused_computation.1.clone | custom fusion | bytes 1966400 | tf_op jit(solution)/shard_map/jit(_take)/gather | solution.py:64
  10.2 8.8 %collective-permute-start.1 = (bf16[80,6144]{1,0:T(8,128)(2,1)S(1)}, bf16[80,6144]{1,0:T(8,128)(2,1)}, u32[]{:S(2)}, u32[]{:S(2)}) collective-permute-start(bf16[80,6144]{1,0:T(8,128)(2,1)S(1)} %select_select_fusion), channel_id=1, source_target_pairs={{1,0},{2,1},{3,2},{4,3},{5,4},{6,5},{7,6},{8,7},{9,8},{10,9},{11,1... | collective-permute-start | bytes 2949128 | tf_op jit(solution)/shard_map/ppermute | solution.py:13
  19.0 4.7 %gather_fusion.4 = bf16[80,6144]{1,0:T(8,128)(2,1)S(1)} fusion(bf16[320,6144]{1,0:T(8,128)(2,1)} %param.6, s32[1024]{0:T(1024)S(1)} %pad_clamp_fusion.4), kind=kCustom, calls=%fused_computation.clone | custom fusion | bytes 1966400 | tf_op jit(solution)/shard_map/jit(_take)/gather | solution.py:64
  24.4 1.1 select_select_fusion.1
  25.5 2.1 %collective-permute-start = (bf16[80,6144]{1,0:T(8,128)(2,1)}, bf16[80,6144]{1,0:T(8,128)(2,1)}, u32[]{:S(2)}, u32[]{:S(2)}) collective-permute-start(bf16[80,6144]{1,0:T(8,128)(2,1)} %select_select_fusion.1), channel_id=1, source_target_pairs={{0,1},{1,2},{2,3},{3,4},{4,5},{5,6},{6,7},{7,8},{8,9},{9,10},{10,1... | collective-permute-start | bytes 2949128 | tf_op jit(solution)/shard_map/ppermute | solution.py:13
  27.6 1.4 %gather_fusion.2 = s32[160]{0:T(256)S(1)} fusion(s32[2560]{0:T(1024)S(1)} %copy-done, s32[1024]{0:T(1024)S(1)} %pad_clamp_fusion.1), kind=kCustom, calls=%fused_computation.4 | custom fusion | bytes 1920 | tf_op jit(solution)/shard_map/gather | solution.py:63
  29.7 6.2 %gather_fusion.3 = bf16[160,6144]{1,0:T(8,128)(2,1)S(1)} fusion(bf16[320,6144]{1,0:T(8,128)(2,1)} %param.6, s32[1024]{0:T(1024)S(1)} %pad_clamp_fusion), kind=kCustom, calls=%fused_computation.5 | custom fusion | bytes 3932800 | tf_op jit(solution)/shard_map/jit(_take)/gather | solution.py:64
  36.0 1.2 compare_and_fusion.3
  37.2 1.6 %collective-permute-done = bf16[80,6144]{1,0:T(8,128)(2,1)} collective-permute-done((bf16[80,6144]{1,0:T(8,128)(2,1)}, bf16[80,6144]{1,0:T(8,128)(2,1)}, u32[]{:S(2)}, u32[]{:S(2)}) %collective-permute-start) | collective-permute-done | bytes 983072 | tf_op jit(solution)/shard_map/ppermute | solution.py:13
  38.8 3.5 %select_bitcast_fusion = bf16[20,8,48,128]{3,1,2,0:T(8,128)(2,1)S(1)} fusion(bf16[160,6144]{1,0:T(8,128)(2,1)S(1)} %gather_fusion.3, bf16[80,6144]{1,0:T(8,128)(2,1)} %collective-permute-done.1, bf16[80,6144]{1,0:T(8,128)(2,1)} %collective-permute-done, pred[160]{0:T(512)(128)(4,1)S(1)} %get-tuple-element.71, pred[160]{0:T(512)(128)(4,1)S(1)} %get-tuple-element.82, ...), kind=kLoop, calls=%fused_computation.22 | loop fusion | flops 3932160 | bytes 5898880
  42.7 1.8 %copy.18 = bf16[160,3,16,1,128]{4,0,3,1,2:T(8,128)(2,1)} copy(bf16[160,3,16,1,128]{4,2,1,0,3:T(8,128)(2,1)S(1)} %bitcast.76) | data formatting | bytes 3932160 | tf_op jit(solution)/shard_map/reshape | solution.py:85
  44.5 8.6 %all-to-all-start = ((bf16[160,3,16,1,128]{4,0,3,1,2:T(8,128)(2,1)}), bf16[160,3,16,1,128]{4,0,3,1,2:T(8,128)(2,1)S(1)}, u32[]{:S(2)}, u32[]{:S(2)}) async-start(bf16[160,3,16,1,128]{4,0,3,1,2:T(8,128)(2,1)} %copy.18), calls=%async_computation | async-start | bytes 3932160 | tf_op jit(solution)/shard_map/all_to_all | solution.py:87
  53.1 46.3 %all-to-all-done = bf16[160,3,16,1,128]{4,0,3,1,2:T(8,128)(2,1)S(1)} async-done(((bf16[160,3,16,1,128]{4,0,3,1,2:T(8,128)(2,1)}), bf16[160,3,16,1,128]{4,0,3,1,2:T(8,128)(2,1)S(1)}, u32[]{:S(2)}, u32[]{:S(2)}) %all-to-all-start) | async-done | bytes 1966112 | tf_op jit(solution)/shard_map/all_to_all | solution.py:87
  99.7 13.7 %while.10 = (s32[]{:T(128)}, bf16[5,512,1,128]{3,1,2,0:T(8,128)(2,1)S(1)}, bf16[5,512,1,128]{3,1,2,0:T(8,128)(2,1)S(1)}, bf16[2560,1,128]{2,0,1:T(8,128)(2,1)S(1)}, bf16[2560,1,128]{2,0,1:T(8,128)(2,1)S(1)}, /*index=5*/s32[]{:T(128)}) while((s32[]{:T(128)}, bf16[5,512,1,128]{3,1,2,0:T(8,128)(2,1)S(1)}, bf16[5,512,1,128]{3,1,2,0:T(8,128)(2,1)S(1)}, ...), condition=%wide.region_5.7_spmd, body=%wide.region_2.6_spmd.sunk | while | flops 679083008 | bytes 17311820 | solution.py:41
  99.7 0.9 fusion.37
  100.6 0.8 fusion.38
  101.5 1.0 fusion.39
  102.4 0.9 fusion.37
  103.4 0.8 fusion.38
  104.2 1.0 fusion.39
  105.2 0.9 fusion.37
  107.0 1.0 fusion.39
  107.9 0.9 fusion.37
  109.7 1.0 fusion.39
  110.7 0.9 fusion.37
  112.5 1.0 fusion.39
  113.9 1.1 reduce.4
  115.2 24.8 %all_to_all.30 = bf16[16,2,10240]{2,1,0:T(2,128)(2,1)S(1)} all-to-all(bf16[16,2,10240]{2,1,0:T(2,128)(2,1)S(1)} %reshape.208), channel_id=1, replica_groups=mesh['dp'=32,'seq'=16] {'seq'}, dimensions={0} | all-to-all | bytes 1310720 | tf_op jit(solution)/shard_map/all_to_all | solution.py:89
  141.1 1.0 copy.27
  (30 shorter events, 6.9 us)
Async XLA Ops:
  10.2 27.0 %collective-permute-start.1 = (bf16[80,6144]{1,0:T(8,128)(2,1)S(1)}, bf16[80,6144]{1,0:T(8,128)(2,1)}, u32[]{:S(2)}, u32[]{:S(2)}) collective-permute-start(bf16[80,6144]{1,0:T(8,128)(2,1)S(1)} %select_select_fusion), channel_id=1, source_target_pairs={{1,0},{2,1},{3,2},{4,3},{5,4},{6,5},{7,6},{8,7},{9,8},{10,9},{11,1... | collective-permute-start | bytes 2949128 | tf_op jit(solution)/shard_map/ppermute | solution.py:13
  23.7 4.0 %copy-start = (s32[2560]{0:T(1024)S(1)}, s32[2560]{0:T(1024)}, u32[]{:S(2)}) copy-start(s32[2560]{0:T(1024)} %param.7) | copy-start | bytes 30724
  25.5 13.3 %collective-permute-start = (bf16[80,6144]{1,0:T(8,128)(2,1)}, bf16[80,6144]{1,0:T(8,128)(2,1)}, u32[]{:S(2)}, u32[]{:S(2)}) collective-permute-start(bf16[80,6144]{1,0:T(8,128)(2,1)} %select_select_fusion.1), channel_id=1, source_target_pairs={{0,1},{1,2},{2,3},{3,4},{4,5},{5,6},{6,7},{7,8},{8,9},{9,10},{10,1... | collective-permute-start | bytes 2949128 | tf_op jit(solution)/shard_map/ppermute | solution.py:13
  44.5 54.9 %all-to-all-start = ((bf16[160,3,16,1,128]{4,0,3,1,2:T(8,128)(2,1)}), bf16[160,3,16,1,128]{4,0,3,1,2:T(8,128)(2,1)S(1)}, u32[]{:S(2)}, u32[]{:S(2)}) async-start(bf16[160,3,16,1,128]{4,0,3,1,2:T(8,128)(2,1)} %copy.18), calls=%async_computation | async-start | bytes 3932160 | tf_op jit(solution)/shard_map/all_to_all | solution.py:87
where the time goes:
time: 143 us; the launch traced here: 142 us
  waiting for transfers between devices  47.9 us (33%)
  local copies, waits for them, and re-layouts  25.5 us (18%)
  blocking collectives  24.8 us (17%)
  starting transfers between devices  19.5 us (14%)
  other arithmetic  14.6 us (10%)
  matrix products  9.44 us (7%)
    all_to_all x1, waiting for transfers between devices, local(): lax.all_to_all(grouped, 'seq', split_axis=2, concat_axis=0, tiled=True)  46.3 us
    all_to_all x1, blocking collectives, local(): lax.all_to_all(attended, 'seq', split_axis=0, concat_axis=1, tiled=True)  24.8 us
    gather x3, local copies, waits for them, and re-layouts, select_rows(): picked = jnp.take(projected, within, axis=0)  15.6 us
    ppermute x2, starting transfers between devices, passed_along(): return lax.ppermute(block, axis, route)  10.9 us
    all_to_all x1, starting transfers between devices, local(): lax.all_to_all(grouped, 'seq', split_axis=2, concat_axis=0, tiled=True)  8.62 us
    dot_general x5, matrix products, one_block(): jnp.einsum('hqk,khd->qhd', weights.astype(jnp.bfloat16), value_rows, pref...  4.8 us
    gather x3, local copies, waits for them, and re-layouts, select_rows(): within = jnp.clip(kept_index[bounded] - first_token, 0, tile_rows - 1)  4.71 us
    dot_general x5, matrix products, one_block(): jnp.einsum('qhd,khd->hqk', query_block, key_rows, preferred_element_type=...  4.64 us
  transfers between devices with their start and end apart: 3, of which 2 were waited for; matrix products, arithmetic and copies ran while one was open for 11% of the time, Pallas kernels for 0%

commit v1 on v0

v1 whole, which is shorter than its diff:
```python
import functools

import jax
import jax.numpy as jnp
from jax import lax
from jax.experimental import pallas as pl
from jax.experimental.pallas import tpu as pltpu
from jax.sharding import PartitionSpec as P

H = 16
HD = 128
LOG2E = 1.4426950408889634
VMEM_BYTES = 50 * 1024 * 1024


def select_kernel(index_ref, q_ref, k_ref, v_ref, own_ref, left_ref, right_ref, choice):
    tokens = q_ref.shape[0]
    spill = left_ref.shape[1]
    rows = own_ref.shape[1]
    heads = own_ref.shape[0]

    @pl.when(pl.program_id(0) == 0)
    def _():
        token = lax.broadcasted_iota(jnp.int32, (tokens, choice.shape[0]), 0)
        hits = jnp.where(token == index_ref[...], 1.0, 0.0)
        choice[...] = jnp.transpose(hits).astype(jnp.bfloat16)

    for c, ref in enumerate((q_ref, k_ref, v_ref)):
        picked = jnp.dot(choice[...], ref[...], preferred_element_type=jnp.float32)
        picked = picked.astype(jnp.bfloat16)
        for h in range(heads):
            block = picked[:, h * HD : (h + 1) * HD]
            place = slice(c * HD, (c + 1) * HD)
            left_ref[h, :, place] = block[:spill]
            own_ref[h, :, place] = block[spill : spill + rows]
            right_ref[h, :, place] = block[spill + rows :]


def select_rows(projected, index_row, shard_rows, spill_rows):
    tokens, width = projected.shape
    groups = 4
    heads = H // groups
    slots = shard_rows + 2 * spill_rows

    def columns(c):
        return pl.BlockSpec((tokens, heads * HD), lambda g: (0, c * groups + g))

    def by_head(rows):
        return pl.BlockSpec((heads, rows, 3 * HD), lambda g: (g, 0, 0))

    def result(rows):
        return jax.ShapeDtypeStruct((H, rows, 3 * HD), projected.dtype)

    return pl.pallas_call(
        select_kernel,
        out_shape=(result(shard_rows), result(spill_rows), result(spill_rows)),
        grid=(groups,),
        in_specs=[pl.BlockSpec((1, slots), lambda g: (0, 0)), columns(0), columns(1), columns(2)],
        out_specs=(by_head(shard_rows), by_head(spill_rows), by_head(spill_rows)),
        scratch_shapes=[pltpu.VMEM((slots, tokens), jnp.bfloat16)],
        compiler_params=pltpu.CompilerParams(vmem_limit_bytes=VMEM_BYTES),
    )(index_row, projected, projected, projected)


def attend_kernel(q_ref, k_ref, v_ref, out_ref, *, block):
    key_rows = k_ref[...]
    ones = jnp.ones(v_ref.shape, v_ref.dtype)
    value_rows = jnp.concatenate([v_ref[...], ones], axis=1)
    scale = HD ** (-0.5) * LOG2E
    for start in range(0, q_ref.shape[0], block):
        queries = q_ref[start : start + block, :]
        scores = lax.dot_general(
            queries, key_rows, (((1,), (1,)), ((), ())), preferred_element_type=jnp.float32
        )
        row_max = jnp.max(scores, axis=-1, keepdims=True)
        weights = jnp.exp2((scores - row_max) * scale).astype(jnp.bfloat16)
        mixed = jnp.dot(weights, value_rows, preferred_element_type=jnp.float32)
        out_ref[start : start + block, :] = (mixed[:, :HD] / mixed[:, HD:]).astype(out_ref.dtype)


def attend(triples):
    total = triples.shape[0]

    def columns(c):
        return pl.BlockSpec((total, HD), lambda i: (0, c))

    return pl.pallas_call(
        functools.partial(attend_kernel, block=256),
        out_shape=jax.ShapeDtypeStruct((total, HD), triples.dtype),
        grid=(1,),
        in_specs=[columns(0), columns(1), columns(2)],
        out_specs=pl.BlockSpec((total, HD), lambda i: (0, 0)),
        compiler_params=pltpu.CompilerParams(vmem_limit_bytes=VMEM_BYTES),
    )(triples, triples, triples)


def passed_along(block, axis, distance):
    devices = range(lax.axis_size(axis))
    route = [(i - distance, i) for i in devices if i - distance in devices]
    return lax.ppermute(block, axis, route)


def local(projected, kept_index):
    device_count = lax.axis_size("seq")
    device_place = lax.axis_index("seq")
    tile_rows = projected.shape[0]
    kept_total = kept_index.shape[0]
    shard_rows = kept_total // device_count
    spill_rows = tile_rows // 4
    slots = shard_rows + 2 * spill_rows
    padded = jnp.pad(kept_index - device_place * tile_rows, (spill_rows, spill_rows), constant_values=-1)
    index_row = lax.dynamic_slice(padded, (device_place * shard_rows,), (slots,))[None, :]
    own, left_rows, right_rows = select_rows(projected, index_row, shard_rows, spill_rows)
    from_left = passed_along(right_rows, "seq", 1)
    from_right = passed_along(left_rows, "seq", -1)
    shard_data = own + jnp.concatenate([from_left, from_right], axis=1)
    triples = lax.all_to_all(shard_data, "seq", split_axis=0, concat_axis=0, tiled=True)
    attended = attend(triples.reshape(kept_total, 3 * HD))
    by_shard = attended.reshape(device_count, shard_rows, HD)
    returned = lax.all_to_all(by_shard, "seq", split_axis=0, concat_axis=0, tiled=True)
    return jnp.transpose(returned, (1, 0, 2)).reshape(shard_rows, H * HD)


def solution(mesh):
    return jax.shard_map(
        local,
        mesh=mesh,
        in_specs=(P(("dp", "seq"), None), P("dp")),
        out_specs=P(("dp", "seq"), None),
        check_vma=False,
    )
```

time: 143 us -> 117 us (0.82)
  blocking collectives: 24.8 us -> 80.7 us
  waiting for transfers between devices: 47.9 us -> 10.7 us
  local copies, waits for them, and re-layouts: 25.5 us -> 0.99 us
  other arithmetic: 14.6 us -> 1.26 us
  Pallas kernels: 0 us -> 12.8 us
  matrix products: 9.44 us -> 0 us
  starting transfers between devices: 19.5 us -> 10.1 us
    all_to_all x1 -> x2, blocking collectives: 24.8 us -> 80.7 us  [the longest x1 57.8 us: local(): lax.all_to_all(shard_data, 'seq', split_axis=0, concat_axis=0, tiled=True)]
    all_to_all x1 -> x0, waiting for transfers between devices: 46.3 us -> none  [local(): lax.all_to_all(grouped, 'seq', split_axis=2, concat_axis=0, tiled=True)]
    gather x6 -> x0, local copies, waits for them, and re-layouts: 20.3 us -> none  [the longest x3 15.6 us: select_rows(): picked = jnp.take(projected, within, axis=0)]
    pallas_call x0 -> x2, Pallas kernels: none -> 12.8 us  [the longest x1 8.13 us: attend(): pl.pallas_call(functools.partial(attend_kernel, block=256), out_shape=jax...]
    dot_general x10 -> x0, matrix products: 9.44 us -> none  [the longest x5 4.8 us: one_block(): jnp.einsum('hqk,khd->qhd', weights.astype(jnp.bfloat16), value_rows, pref...]
    ppermute x2, waiting for transfers between devices: 1.57 us -> 10.7 us  [passed_along(): return lax.ppermute(block, axis, route)]
    all_to_all x1 -> x0, starting transfers between devices: 8.62 us -> none  [local(): lax.all_to_all(grouped, 'seq', split_axis=2, concat_axis=0, tiled=True)]
    reduce_sum x6 -> x0, other arithmetic: 5.57 us -> none  [the longest x5 4.22 us: one_block(): totals = jnp.sum(weights, axis=-1)]
  transfers between devices with their start and end apart: 3 -> 2, of which waited for: 2 -> 2; matrix products, arithmetic and copies ran while one was open for 11% -> 0% of each run, Pallas kernels for 0% -> 0%
where the time goes in v1:
time: 117 us
  blocking collectives  80.7 us (69%)
  Pallas kernels  12.8 us (11%)
  waiting for transfers between devices  10.7 us (9%)
  starting transfers between devices  10.1 us (9%)
  other arithmetic  1.26 us (1%)
    all_to_all x1, blocking collectives, local(): lax.all_to_all(shard_data, 'seq', split_axis=0, concat_axis=0, tiled=True)  57.8 us
    all_to_all x1, blocking collectives, local(): lax.all_to_all(by_shard, 'seq', split_axis=0, concat_axis=0, tiled=True)  22.9 us
    ppermute x2, waiting for transfers between devices, passed_along(): return lax.ppermute(block, axis, route)  10.7 us
    ppermute x2, starting transfers between devices, passed_along(): return lax.ppermute(block, axis, route)  10.1 us
    pallas_call x1, Pallas kernels, attend(): pl.pallas_call(functools.partial(attend_kernel, block=256), out_shape=jax...  8.13 us
    pallas_call x1, Pallas kernels, select_rows(): pl.pallas_call(select_kernel, out_shape=(result(shard_rows), result(spill...  4.67 us
  transfers between devices with their start and end apart: 2, of which 2 were waited for; matrix products, arithmetic and copies ran while one was open for 0% of the time, Pallas kernels for 0%

profile of v1, /device:TPU:1, one launch (start us, length us, event | category | flops | bytes accessed | tf_op | source)
XLA Modules:
  0.0 116.6 jit_solution(5823976922182325218)
XLA Ops:
  0.0 0.7 broadcast_subtract_fusion
  0.7 0.1 pad_dynamic-slice_fusion
  0.8 4.7 %shard_map.28 = (bf16[16,160,384]{2,1,0:T(8,128)(2,1)S(1)}, bf16[16,80,384]{2,1,0:T(8,128)(2,1)S(1)}, bf16[16,80,384]{2,1,0:T(8,128)(2,1)S(1)}) custom-call(s32[1,320]{1,0:T(1,128)S(1)} %broadcast_in_dim.3.index_ref, bf16[320,6144]{1,0:T(8,128)(2,1)} %v_ref.1, bf16[320,6144]{1,0:T(8,128)(2,1)} %v_ref.1, bf16[320,6144]{1,0:T(8,128)(2,1)} %v_ref.1), custom_call_target="tpu_custom_call" | custom-call | tf_op jit(solution)/shard_map/pallas_call | solution.py:54
  5.5 5.4 %collective-permute-start = (bf16[16,80,384]{2,1,0:T(8,128)(2,1)S(1)}, bf16[16,80,384]{2,1,0:T(8,128)(2,1)S(1)}, u32[]{:S(2)}, u32[]{:S(2)}) collective-permute-start(bf16[16,80,384]{2,1,0:T(8,128)(2,1)S(1)} %get-tuple-element.9), channel_id=1, source_target_pairs={{0,1},{1,2},{2,3},{3,4},{4,5},{5,6},{6,7},{7,8},{8,9},{9,10},{10,1... | collective-permute-start | bytes 2949128 | tf_op jit(solution)/shard_map/ppermute | solution.py:100
  10.9 4.7 %collective-permute-start.1 = (bf16[16,80,384]{2,1,0:T(8,128)(2,1)S(1)}, bf16[16,80,384]{2,1,0:T(8,128)(2,1)S(1)}, u32[]{:S(2)}, u32[]{:S(2)}) collective-permute-start(bf16[16,80,384]{2,1,0:T(8,128)(2,1)S(1)} %get-tuple-element.10), channel_id=1, source_target_pairs={{1,0},{2,1},{3,2},{4,3},{5,4},{6,5},{7,6},{8,7},{9,8},{10,9},{11,1... | collective-permute-start | bytes 2949128 | tf_op jit(solution)/shard_map/ppermute | solution.py:100
  15.6 6.3 %collective-permute-done = bf16[16,80,384]{2,1,0:T(8,128)(2,1)S(1)} collective-permute-done((bf16[16,80,384]{2,1,0:T(8,128)(2,1)S(1)}, bf16[16,80,384]{2,1,0:T(8,128)(2,1)S(1)}, u32[]{:S(2)}, u32[]{:S(2)}) %collective-permute-start) | collective-permute-done | bytes 983072 | tf_op jit(solution)/shard_map/ppermute | solution.py:100
  21.9 4.4 %collective-permute-done.1 = bf16[16,80,384]{2,1,0:T(8,128)(2,1)S(1)} collective-permute-done((bf16[16,80,384]{2,1,0:T(8,128)(2,1)S(1)}, bf16[16,80,384]{2,1,0:T(8,128)(2,1)S(1)}, u32[]{:S(2)}, u32[]{:S(2)}) %collective-permute-start.1) | collective-permute-done | bytes 983072 | tf_op jit(solution)/shard_map/ppermute | solution.py:100
  26.3 0.6 maximum_add_fusion
  26.8 57.8 %all_to_all.10 = bf16[16,160,384]{2,1,0:T(8,128)(2,1)S(1)} all-to-all(bf16[16,160,384]{2,1,0:T(8,128)(2,1)S(1)} %maximum_add_fusion), channel_id=1, replica_groups=mesh['dp'=32,'seq'=16] {'seq'}, dimensions={0} | all-to-all | bytes 3932160 | tf_op jit(solution)/shard_map/all_to_all | solution.py:117
  84.7 8.1 %shard_map.29 = bf16[2560,128]{1,0:T(8,128)(2,1)S(1)} custom-call(bf16[2560,384]{1,0:T(8,128)(2,1)S(1)} %bitcast.8, bf16[2560,384]{1,0:T(8,128)(2,1)S(1)} %bitcast.9, bf16[2560,384]{1,0:T(8,128)(2,1)S(1)} %bitcast.10), custom_call_target="tpu_custom_call" | custom-call | tf_op jit(solution)/shard_map/pallas_call | solution.py:87
  92.8 22.9 %all_to_all.11 = bf16[16,160,128]{2,1,0:T(8,128)(2,1)S(1)} all-to-all(bf16[16,160,128]{2,1,0:T(8,128)(2,1)S(1)} %bitcast.11), channel_id=1, replica_groups=mesh['dp'=32,'seq'=16] {'seq'}, dimensions={0} | all-to-all | bytes 1310720 | tf_op jit(solution)/shard_map/all_to_all | solution.py:120
  115.7 0.9 copy_bitcast_fusion
  (1 shorter events, 0.0 us)
Async XLA Ops:
  5.5 16.4 %collective-permute-start = (bf16[16,80,384]{2,1,0:T(8,128)(2,1)S(1)}, bf16[16,80,384]{2,1,0:T(8,128)(2,1)S(1)}, u32[]{:S(2)}, u32[]{:S(2)}) collective-permute-start(bf16[16,80,384]{2,1,0:T(8,128)(2,1)S(1)} %get-tuple-element.9), channel_id=1, source_target_pairs={{0,1},{1,2},{2,3},{3,4},{4,5},{5,6},{6,7},{7,8},{8,9},{9,10},{10,1... | collective-permute-start | bytes 2949128 | tf_op jit(solution)/shard_map/ppermute | solution.py:100
  10.9 15.4 %collective-permute-start.1 = (bf16[16,80,384]{2,1,0:T(8,128)(2,1)S(1)}, bf16[16,80,384]{2,1,0:T(8,128)(2,1)S(1)}, u32[]{:S(2)}, u32[]{:S(2)}) collective-permute-start(bf16[16,80,384]{2,1,0:T(8,128)(2,1)S(1)} %get-tuple-element.10), channel_id=1, source_target_pairs={{1,0},{2,1},{3,2},{4,3},{5,4},{6,5},{7,6},{8,7},{9,8},{10,9},{11,1... | collective-permute-start | bytes 2949128 | tf_op jit(solution)/shard_map/ppermute | solution.py:100

commit v2 on v1

v2 whole, which is shorter than its diff:
```python
import functools

import jax
import jax.numpy as jnp
from jax import lax
from jax.experimental import pallas as pl
from jax.experimental.pallas import tpu as pltpu
from jax.sharding import PartitionSpec as P

H = 16
HD = 128
CORES = 2
GROUPS = 4
LOG2E = 1.4426950408889634
VMEM_BYTES = 50 * 1024 * 1024


def choose(device, index_ref, tokens, rows, choice):
    kept = index_ref.shape[0]
    spill = rows // 2
    shift = lax.rem(spill - device * rows + kept, kept)
    index = pltpu.roll(jnp.broadcast_to(index_ref[...].reshape(1, kept), (8, kept)), shift, 1)
    index = index[:1, : 2 * rows] - device * tokens
    token = lax.broadcasted_iota(jnp.int32, (tokens, 2 * rows), 0)
    hits = jnp.transpose(jnp.where(token == index, 1.0, 0.0))
    groups = [hits[i : i + spill] for i in range(0, 2 * rows, spill)]
    odd = lax.rem(device, CORES) == 1
    for i in range(len(groups)):
        chosen = jnp.where(odd, groups[-1 - i], groups[i])
        choice[i * spill : (i + 1) * spill, :] = chosen.astype(jnp.bfloat16)


def select_kernel(place_ref, index_ref, q_ref, k_ref, v_ref, *refs, first):
    *out_refs, choice = refs
    tokens = q_ref.shape[0]

    @pl.when(pl.program_id(0) == 0)
    def _():
        choose(place_ref[0], index_ref, tokens, tokens // 2, choice)

    count = sum(ref.shape[1] for ref in out_refs)
    for c, ref in enumerate((q_ref, k_ref, v_ref)):
        picked = jnp.dot(choice[first : first + count, :], ref[...], preferred_element_type=jnp.float32)
        picked = picked.astype(jnp.bfloat16)
        start = 0
        for out_ref in out_refs:
            heads, rows, _ = out_ref.shape
            for h in range(heads):
                block = picked[start : start + rows, h * HD : (h + 1) * HD]
                out_ref[h, :, c * HD : (c + 1) * HD] = block
            start += rows


def select_rows(place, kept_index, projected, first, counts):
    tokens = projected.shape[0]
    heads = H // GROUPS

    def columns(c):
        return pl.BlockSpec((tokens, heads * HD), lambda g, place: (0, c * GROUPS + g))

    def by_head(rows):
        return pl.BlockSpec((heads, rows, 3 * HD), lambda g, place: (g, 0, 0))

    return pl.pallas_call(
        functools.partial(select_kernel, first=first),
        out_shape=[jax.ShapeDtypeStruct((H, rows, 3 * HD), projected.dtype) for rows in counts],
        grid_spec=pltpu.PrefetchScalarGridSpec(
            num_scalar_prefetch=1,
            grid=(GROUPS,),
            in_specs=[pl.BlockSpec(kept_index.shape, lambda g, place: (0,))] + [columns(c) for c in range(3)],
            out_specs=[by_head(rows) for rows in counts],
            scratch_shapes=[pltpu.VMEM((tokens, tokens), jnp.bfloat16)],
        ),
        compiler_params=pltpu.CompilerParams(vmem_limit_bytes=VMEM_BYTES),
    )(place, kept_index, projected, projected, projected)


def attend_kernel(q_ref, k_ref, v_ref, out_ref, *, block):
    key_rows = k_ref[...]
    ones = jnp.ones(v_ref.shape, v_ref.dtype)
    value_rows = jnp.concatenate([v_ref[...], ones], axis=1)
    scale = HD ** (-0.5) * LOG2E
    starts = range(0, q_ref.shape[0], block)

    half = block // 4

    def scores_of(start):
        middle, last = start + 2 * half, start + 3 * half
        queries = jnp.concatenate(
            [q_ref[start:middle, :], q_ref[last : last + half, :], q_ref[middle:last, :]], axis=0
        )
        return lax.dot_general(
            queries, key_rows, (((1,), (1,)), ((), ())), preferred_element_type=jnp.float32
        )

    def weights_of(scores):
        row_max = jnp.max(scores, axis=-1, keepdims=True)
        return jnp.exp2((scores - row_max) * scale).astype(jnp.bfloat16)

    def write(start, weights):
        mixed = jnp.dot(weights, value_rows, preferred_element_type=jnp.float32)
        out_ref[start : start + block, :] = (mixed[:, :HD] / mixed[:, HD:]).astype(out_ref.dtype)

    scores = scores_of(0)
    weights = None
    for start in starts:
        later = scores_of(start + block) if start + block < starts.stop else None
        newer = weights_of(scores)
        if weights is not None:
            write(start - block, weights)
        scores, weights = later, newer
    write(starts[-1], weights)


def attend(triples, shard_rows):
    total = triples.shape[0]

    def columns(c):
        return pl.BlockSpec((total, HD), lambda i: (0, c))

    return pl.pallas_call(
        functools.partial(attend_kernel, block=CORES * shard_rows),
        out_shape=jax.ShapeDtypeStruct((total, HD), triples.dtype),
        grid=(1,),
        in_specs=[columns(0), columns(1), columns(2)],
        out_specs=pl.BlockSpec((total, HD), lambda i: (0, 0)),
        compiler_params=pltpu.CompilerParams(vmem_limit_bytes=VMEM_BYTES),
    )(triples, triples, triples)


def local(projected, kept_index):
    device_count = lax.axis_size("seq")
    place = lax.axis_index("seq").astype(jnp.int32)[None]
    kept_total = kept_index.shape[0]
    shard_rows = kept_total // device_count
    spill_rows = projected.shape[0] // 4
    across = [(i, i - 1 + 2 * (i % 2)) for i in range(1, device_count - 1)]
    within = [(i, i ^ 1) for i in range(device_count)]
    (inter,) = select_rows(place, kept_index, projected, 0, [spill_rows])
    from_across = lax.ppermute(inter, "seq", across)
    own, intra = select_rows(place, kept_index, projected, spill_rows, [shard_rows, spill_rows])
    from_within = lax.ppermute(intra, "seq", within)
    shard_data = own + jnp.concatenate([from_across, from_within], axis=1)
    triples = lax.all_to_all(shard_data, "seq", split_axis=0, concat_axis=0, tiled=True)
    attended = attend(triples.reshape(kept_total, 3 * HD), shard_rows)
    by_shard = attended.reshape(device_count, shard_rows, HD)
    returned = lax.all_to_all(by_shard, "seq", split_axis=0, concat_axis=0, tiled=True)
    return jnp.transpose(returned, (1, 0, 2)).reshape(shard_rows, H * HD)


def solution(mesh):
    return jax.shard_map(
        local,
        mesh=mesh,
        in_specs=(P(("dp", "seq"), None), P("dp")),
        out_specs=P(("dp", "seq"), None),
        check_vma=False,
    )
```

time: 117 us -> 113 us (0.966)
  waiting for transfers between devices: 10.7 us -> 3.24 us
  Pallas kernels: 12.8 us -> 15.7 us
  blocking collectives: 80.7 us -> 82.2 us
    ppermute x2, waiting for transfers between devices: 10.7 us -> 3.24 us  [the longest x1 3.24 us: local(): from_across = lax.ppermute(inter, 'seq', across)]
    pallas_call x2 -> x3, Pallas kernels: 12.8 us -> 15.7 us  [the longest x2 8.17 us: select_rows(): pl.pallas_call(functools.partial(select_kernel, first=first), out_shape=[...]
    all_to_all x1, blocking collectives: 57.8 us -> 59.3 us  [local(): lax.all_to_all(shard_data, 'seq', split_axis=0, concat_axis=0, tiled=True)]
  transfers between devices with their start and end apart: 2 -> 2, of which waited for: 2 -> 1; matrix products, arithmetic and copies ran while one was open for 0% -> 0% of each run, Pallas kernels for 0% -> 4%
where the time goes in v2:
time: 113 us
  blocking collectives  82.2 us (73%)
  Pallas kernels  15.7 us (14%)
  starting transfers between devices  9.49 us (8%)
  waiting for transfers between devices  3.24 us (3%)
  local copies, waits for them, and re-layouts  1.62 us (1%)
    all_to_all x1, blocking collectives, local(): lax.all_to_all(shard_data, 'seq', split_axis=0, concat_axis=0, tiled=True)  59.3 us
    all_to_all x1, blocking collectives, local(): lax.all_to_all(by_shard, 'seq', split_axis=0, concat_axis=0, tiled=True)  22.9 us
    pallas_call x2, Pallas kernels, select_rows(): pl.pallas_call(functools.partial(select_kernel, first=first), out_shape=[...  8.17 us
    pallas_call x1, Pallas kernels, attend(): pl.pallas_call(functools.partial(attend_kernel, block=CORES * shard_rows)...  7.56 us
    ppermute x1, starting transfers between devices, local(): from_across = lax.ppermute(inter, 'seq', across)  5.39 us
    ppermute x1, starting transfers between devices, local(): from_within = lax.ppermute(intra, 'seq', within)  4.1 us
    ppermute x1, waiting for transfers between devices, local(): from_across = lax.ppermute(inter, 'seq', across)  3.24 us
  transfers between devices with their start and end apart: 2, of which 1 were waited for; matrix products, arithmetic and copies ran while one was open for 0% of the time, Pallas kernels for 4%

profile of v2, /device:TPU:1, one launch (start us, length us, event | category | flops | bytes accessed | tf_op | source)
XLA Modules:
  0.0 112.8 jit_solution(1336959037497608503)
XLA Ops:
  0.0 0.0 copy-start
  0.0 0.7 copy-done
  0.7 3.8 %shard_map.29 = bf16[16,80,384]{2,1,0:T(8,128)(2,1)S(1)} custom-call(s32[1]{0:T(128)} %bitcast.place_ref, s32[2560]{0:T(1024)S(1)} %copy-done, bf16[320,6144]{1,0:T(8,128)(2,1)} %v_ref.3, bf16[320,6144]{1,0:T(8,128)(2,1)} %v_ref.3, bf16[320,6144]{1,0:T(8,128)(2,1)} %v_ref.3), custom_call_target="tpu_custom_call" | custom-call | tf_op jit(solution)/shard_map/pallas_call | solution.py:64
  4.5 5.4 %collective-permute-start = (bf16[16,80,384]{2,1,0:T(8,128)(2,1)S(1)}, bf16[16,80,384]{2,1,0:T(8,128)(2,1)S(1)}, u32[]{:S(2)}, u32[]{:S(2)}) collective-permute-start(bf16[16,80,384]{2,1,0:T(8,128)(2,1)S(1)} %shard_map.29), channel_id=1, source_target_pairs={{1,2},{2,1},{3,4},{4,3},{5,6},{6,5},{7,8},{8,7},{9,10},{10,9},{11,... | collective-permute-start | bytes 2949128 | tf_op jit(solution)/shard_map/ppermute | solution.py:140
  9.9 4.4 %shard_map.28 = (bf16[16,160,384]{2,1,0:T(8,128)(2,1)S(1)}, bf16[16,80,384]{2,1,0:T(8,128)(2,1)S(1)}) custom-call(s32[1]{0:T(128)} %bitcast.place_ref, s32[2560]{0:T(1024)S(1)} %copy-done, bf16[320,6144]{1,0:T(8,128)(2,1)} %v_ref.3, bf16[320,6144]{1,0:T(8,128)(2,1)} %v_ref.3, bf16[320,6144]{1,0:T(8,128)(2,1)} %v_ref.3), custom_call_target="tpu_custom_call" | custom-call | tf_op jit(solution)/shard_map/pallas_call | solution.py:64
  14.3 4.1 %collective-permute-start.1 = (bf16[16,80,384]{2,1,0:T(8,128)(2,1)S(1)}, bf16[16,80,384]{2,1,0:T(8,128)(2,1)S(1)}, u32[]{:S(2)}, u32[]{:S(2)}) collective-permute-start(bf16[16,80,384]{2,1,0:T(8,128)(2,1)S(1)} %get-tuple-element.8), channel_id=1, source_target_pairs={{0,1},{1,0},{2,3},{3,2},{4,5},{5,4},{6,7},{7,6},{8,9},{9,8},{10,11... | collective-permute-start | bytes 2949128 | tf_op jit(solution)/shard_map/ppermute | solution.py:142
  18.4 3.2 %collective-permute-done = bf16[16,80,384]{2,1,0:T(8,128)(2,1)S(1)} collective-permute-done((bf16[16,80,384]{2,1,0:T(8,128)(2,1)S(1)}, bf16[16,80,384]{2,1,0:T(8,128)(2,1)S(1)}, u32[]{:S(2)}, u32[]{:S(2)}) %collective-permute-start) | collective-permute-done | bytes 983072 | tf_op jit(solution)/shard_map/ppermute | solution.py:140
  21.6 0.0 collective-permute-done.1
  21.6 0.5 maximum_add_fusion
  22.1 59.3 %all_to_all.10 = bf16[16,160,384]{2,1,0:T(8,128)(2,1)S(1)} all-to-all(bf16[16,160,384]{2,1,0:T(8,128)(2,1)S(1)} %maximum_add_fusion), channel_id=1, replica_groups=mesh['dp'=32,'seq'=16] {'seq'}, dimensions={0} | all-to-all | bytes 3932160 | tf_op jit(solution)/shard_map/all_to_all | solution.py:144
  81.4 7.6 %shard_map.30 = bf16[2560,128]{1,0:T(8,128)(2,1)S(1)} custom-call(bf16[2560,384]{1,0:T(8,128)(2,1)S(1)} %bitcast.9, bf16[2560,384]{1,0:T(8,128)(2,1)S(1)} %bitcast.10, bf16[2560,384]{1,0:T(8,128)(2,1)S(1)} %bitcast.11), custom_call_target="tpu_custom_call" | custom-call | tf_op jit(solution)/shard_map/pallas_call | solution.py:121
  89.0 22.9 %all_to_all.11 = bf16[16,160,128]{2,1,0:T(8,128)(2,1)S(1)} all-to-all(bf16[16,160,128]{2,1,0:T(8,128)(2,1)S(1)} %bitcast.12), channel_id=1, replica_groups=mesh['dp'=32,'seq'=16] {'seq'}, dimensions={0} | all-to-all | bytes 1310720 | tf_op jit(solution)/shard_map/all_to_all | solution.py:147
  111.9 0.9 copy_bitcast_fusion
Async XLA Ops:
  0.0 0.7 copy-start
  4.5 17.2 %collective-permute-start = (bf16[16,80,384]{2,1,0:T(8,128)(2,1)S(1)}, bf16[16,80,384]{2,1,0:T(8,128)(2,1)S(1)}, u32[]{:S(2)}, u32[]{:S(2)}) collective-permute-start(bf16[16,80,384]{2,1,0:T(8,128)(2,1)S(1)} %shard_map.29), channel_id=1, source_target_pairs={{1,2},{2,1},{3,4},{4,3},{5,6},{6,5},{7,8},{8,7},{9,10},{10,9},{11,... | collective-permute-start | bytes 2949128 | tf_op jit(solution)/shard_map/ppermute | solution.py:140
  14.3 7.4 %collective-permute-start.1 = (bf16[16,80,384]{2,1,0:T(8,128)(2,1)S(1)}, bf16[16,80,384]{2,1,0:T(8,128)(2,1)S(1)}, u32[]{:S(2)}, u32[]{:S(2)}) collective-permute-start(bf16[16,80,384]{2,1,0:T(8,128)(2,1)S(1)} %get-tuple-element.8), channel_id=1, source_target_pairs={{0,1},{1,0},{2,3},{3,2},{4,5},{5,4},{6,7},{7,6},{8,9},{9,8},{10,11... | collective-permute-start | bytes 2949128 | tf_op jit(solution)/shard_map/ppermute | solution.py:142

commit v3 on v2

v3 whole, which is shorter than its diff:
```python
import functools

import jax
import jax.numpy as jnp
from jax import lax
from jax.experimental import pallas as pl
from jax.experimental.pallas import tpu as pltpu
from jax.sharding import PartitionSpec as P

H = 16
HD = 128
CORES = 2
NEAR = 4
LOG2E = 1.4426950408889634
VMEM_BYTES = 50 * 1024 * 1024


def pick(device, index_ref, start, tokens, count):
    kept = index_ref.shape[0]
    shift = lax.rem(2 * kept - start, kept)
    index = pltpu.roll(jnp.broadcast_to(index_ref[...].reshape(1, kept), (8, kept)), shift, 1)
    index = (index[:, :128] - device * tokens).astype(jnp.float32)
    column = jnp.transpose(index)[:count, :1]
    token = lax.broadcasted_iota(jnp.int32, (count, tokens), 1).astype(jnp.float32)
    return jnp.where(token == column, 1.0, 0.0).astype(jnp.bfloat16)


def spill_kernel(index_ref, tile_ref, out_ref, columns, sems):
    heads, spill, _ = out_ref.shape
    tokens = tile_ref.shape[0]
    kinds, _, width = columns.shape
    copies = []
    for c in range(kinds):
        at = pl.ds(c * width, width)
        copies.append(pltpu.make_async_copy(tile_ref.at[:, at], columns.at[c], sems.at[c]))
        copies[-1].start()
    device = lax.axis_index("seq")
    odd = lax.rem(device, CORES)
    start = (2 * device + odd * 2 + (1 - odd) * -1) * spill
    choice = pick(device, index_ref, start, tokens, spill)
    for c in range(kinds):
        copies[c].wait()
        picked = jnp.dot(choice, columns[c], preferred_element_type=jnp.float32)
        picked = picked.astype(jnp.bfloat16)
        for h in range(heads):
            out_ref[h, :, c * HD : (c + 1) * HD] = picked[:, h * HD : (h + 1) * HD]


def select_spill(kept_index, projected, spill_rows):
    tokens = projected.shape[0]
    vmem = pl.BlockSpec(memory_space=pltpu.VMEM)
    return pl.pallas_call(
        spill_kernel,
        out_shape=jax.ShapeDtypeStruct((H, spill_rows, 3 * HD), projected.dtype),
        in_specs=[vmem, pl.BlockSpec(memory_space=pltpu.HBM)],
        out_specs=vmem,
        scratch_shapes=[
            pltpu.VMEM((3, tokens, H * HD), projected.dtype),
            pltpu.SemaphoreType.DMA((3,)),
        ],
        compiler_params=pltpu.CompilerParams(vmem_limit_bytes=VMEM_BYTES),
    )(kept_index, projected)


def select_kernel(index_ref, q_ref, k_ref, v_ref, *refs, groups, parts):
    *out_refs, choice = refs
    tokens = q_ref.shape[0]
    spill = tokens // 4

    @pl.when(pl.program_id(0) == 0)
    def _():
        device = lax.axis_index("seq")
        odd = lax.rem(device, CORES)
        for i, group in enumerate(groups):
            ahead = odd * (2 - group) + (1 - odd) * (group - 1)
            start = (2 * device + ahead) * spill
            choice[i * spill : (i + 1) * spill, :] = pick(device, index_ref, start, tokens, spill)

    for c, ref in enumerate((q_ref, k_ref, v_ref)):
        picked = jnp.dot(choice[...], ref[...], preferred_element_type=jnp.float32)
        picked = picked.astype(jnp.bfloat16)
        for out_ref, (start, rows, columns) in zip(out_refs, parts):
            if c not in columns:
                continue
            at = columns.index(c) * HD
            for h in range(out_ref.shape[0]):
                out_ref[h, :, at : at + HD] = picked[start : start + rows, h * HD : (h + 1) * HD]


def select_rows(kept_index, projected, groups, parts, steps):
    tokens = projected.shape[0]
    heads = H // steps

    def columns(c):
        return pl.BlockSpec((tokens, heads * HD), lambda g: (0, c * steps + g))

    def by_head(rows, width):
        return pl.BlockSpec((heads, rows, width), lambda g: (g, 0, 0))

    return pl.pallas_call(
        functools.partial(select_kernel, groups=groups, parts=parts),
        out_shape=[
            jax.ShapeDtypeStruct((H, rows, len(cols) * HD), projected.dtype) for _, rows, cols in parts
        ],
        grid=(steps,),
        in_specs=[pl.BlockSpec(kept_index.shape, lambda g: (0,))] + [columns(c) for c in range(3)],
        out_specs=[by_head(rows, len(cols) * HD) for _, rows, cols in parts],
        scratch_shapes=[pltpu.VMEM((len(groups) * tokens // 4, tokens), jnp.bfloat16)],
        compiler_params=pltpu.CompilerParams(vmem_limit_bytes=VMEM_BYTES),
    )(kept_index, projected, projected, projected)


def attend_kernel(triple_ref, *refs, near, shard_rows):
    if near:
        *out_refs, queries_ref, result_ref = refs
    else:
        out_ref, queries_ref, result_ref, zeros_ref, sems = refs
    total = triple_ref.shape[0]
    key_rows = triple_ref[:, HD : 2 * HD]
    ones = jnp.ones((total, HD), triple_ref.dtype)
    value_rows = jnp.concatenate([triple_ref[:, 2 * HD :], ones], axis=1)
    scale = HD ** (-0.5) * LOG2E
    half = shard_rows // 2
    block = 2 * shard_rows
    device = lax.axis_index("seq")
    count = queries_ref.shape[0] // shard_rows

    def shard_of(i):
        return device ^ (i if near else NEAR + i)

    for i in range(count):
        shard = shard_of(i)
        odd = lax.rem(shard, 2)
        for j, at in enumerate((odd, 1 - odd)):
            rows = pl.multiple_of(shard * shard_rows + at * half, 16)
            start = i * shard_rows + j * half
            queries_ref[start : start + half, :] = triple_ref[pl.ds(rows, half), :HD]

    def scores_of(start):
        return lax.dot_general(
            queries_ref[start : start + block, :],
            key_rows,
            (((1,), (1,)), ((), ())),
            preferred_element_type=jnp.float32,
        )

    def weights_of(scores):
        row_max = jnp.max(scores, axis=-1, keepdims=True)
        return jnp.exp2((scores - row_max) * scale).astype(jnp.bfloat16)

    copies = []

    def send(source, shard):
        copies.append(pltpu.make_async_copy(source, out_ref.at[shard], sems.at[len(copies)]))
        copies[-1].start()

    if not near:
        zeros_ref[...] = jnp.zeros_like(zeros_ref)
        for i in range(NEAR):
            send(zeros_ref, device ^ i)

    def write(start, weights):
        mixed = jnp.dot(weights, value_rows, preferred_element_type=jnp.float32)
        result = mixed[:, :HD] / mixed[:, HD:]
        result_ref[start : start + block, :] = result.astype(result_ref.dtype)
        for at in range(start, start + block, shard_rows):
            if near:
                out_refs[at // shard_rows][...] = result_ref[at : at + shard_rows, :]
            else:
                send(result_ref.at[at : at + shard_rows, :], shard_of(at // shard_rows))

    starts = range(0, count * shard_rows, block)
    scores = scores_of(0)
    weights = None
    for start in starts:
        later = scores_of(start + block) if start + block < starts.stop else None
        newer = weights_of(scores)
        if weights is not None:
            write(start - block, weights)
        scores, weights = later, newer
    write(starts[-1], weights)

    for copy in copies:
        copy.wait()


def attend(triples, shard_rows, near):
    total = triples.shape[0]
    shards = total // shard_rows
    whole = pl.BlockSpec(memory_space=pltpu.VMEM)
    if near:
        shape, outs, count, more = (shard_rows, HD), NEAR, NEAR, []
    else:
        more = [pltpu.VMEM((shard_rows, HD), triples.dtype), pltpu.SemaphoreType.DMA((shards,))]
        shape, outs, count = (shards, shard_rows, HD), 1, shards - NEAR
    return pl.pallas_call(
        functools.partial(attend_kernel, near=near, shard_rows=shard_rows),
        out_shape=[jax.ShapeDtypeStruct(shape, triples.dtype)] * outs,
        in_specs=[whole],
        out_specs=[whole if near else pl.BlockSpec(memory_space=pltpu.HBM)] * outs,
        scratch_shapes=[pltpu.VMEM((count * shard_rows, HD), triples.dtype)] * 2 + more,
        compiler_params=pltpu.CompilerParams(vmem_limit_bytes=VMEM_BYTES),
    )(triples)


def assemble_kernel(far_ref, *refs):
    *near_refs, out_ref, sems = refs
    heads = far_ref.shape[0]
    device = lax.axis_index("seq")
    copies = []

    def put(source, head):
        column = pl.multiple_of(head * HD, HD)
        at = len(copies)
        copies.append(pltpu.make_async_copy(source, out_ref.at[:, pl.ds(column, HD)], sems.at[at]))
        copies[-1].start()

    for i in range(NEAR, heads):
        put(far_ref.at[device ^ i], device ^ i)
    for m, ref in enumerate(near_refs):
        put(ref, device ^ m)
    for copy in copies:
        copy.wait()


def assemble(far, near):
    heads, rows, _ = far.shape
    whole = pl.BlockSpec(memory_space=pltpu.VMEM)
    return pl.pallas_call(
        assemble_kernel,
        out_shape=jax.ShapeDtypeStruct((rows, heads * HD), far.dtype),
        in_specs=[whole] * (1 + NEAR),
        out_specs=pl.BlockSpec(memory_space=pltpu.HBM),
        scratch_shapes=[pltpu.SemaphoreType.DMA((heads,))],
        compiler_params=pltpu.CompilerParams(vmem_limit_bytes=VMEM_BYTES),
    )(far, *near)


def local(projected, kept_index):
    device_count = lax.axis_size("seq")
    kept_total = kept_index.shape[0]
    shard_rows = kept_total // device_count
    spill_rows = projected.shape[0] // 4
    across = [(i, i - 1 + 2 * (i % 2)) for i in range(1, device_count - 1)]
    within = [(i, i ^ 1) for i in range(device_count)]
    everything = (0, 1, 2)
    own_parts = [(0, shard_rows, everything), (shard_rows, spill_rows, everything)]
    inter = select_spill(kept_index, projected, spill_rows)
    from_across = lax.ppermute(inter, "seq", across)
    own, intra = select_rows(kept_index, projected, (1, 2, 3), own_parts, 4)
    from_within = lax.ppermute(intra, "seq", within)
    shard_data = own + jnp.concatenate([from_across, from_within], axis=1)
    triples = lax.all_to_all(shard_data, "seq", split_axis=0, concat_axis=0, tiled=True)
    triples = triples.reshape(kept_total, 3 * HD)
    (far,) = attend(triples, shard_rows, False)
    far = lax.all_to_all(far, "seq", split_axis=0, concat_axis=0, tiled=True)
    near = list(attend(triples, shard_rows, True))
    for m in range(1, NEAR):
        near[m] = lax.ppermute(near[m], "seq", [(i, i ^ m) for i in range(device_count)])
    return assemble(far, near)


def solution(mesh):
    return jax.shard_map(
        local,
        mesh=mesh,
        in_specs=(P(("dp", "seq"), None), P("dp")),
        out_specs=P(("dp", "seq"), None),
        check_vma=False,
    )
```

time: 113 us -> 111 us (0.982)
  blocking collectives: 82.2 us -> 59.3 us
  starting transfers between devices: 9.49 us -> 20.9 us
  waiting for transfers between devices: 3.24 us -> 12.6 us
    all_to_all x1 -> x0, blocking collectives: 22.9 us -> none  [local(): lax.all_to_all(by_shard, 'seq', split_axis=0, concat_axis=0, tiled=True)]
    ppermute x0 -> x3, starting transfers between devices: none -> 7.87 us  [local(): lax.ppermute(near[m], 'seq', [(i, i ^ m) for i in range(device_count)])]
    ppermute x0 -> x3, waiting for transfers between devices: none -> 7.83 us  [local(): lax.ppermute(near[m], 'seq', [(i, i ^ m) for i in range(device_count)])]
    all_to_all x0 -> x1, starting transfers between devices: none -> 3.5 us  [local(): far = lax.all_to_all(far, 'seq', split_axis=0, concat_axis=0, tiled=True)]
    all_to_all x0 -> x1, waiting for transfers between devices: none -> 1.64 us  [local(): far = lax.all_to_all(far, 'seq', split_axis=0, concat_axis=0, tiled=True)]
    pallas_call x3 -> x5, Pallas kernels: 15.7 us -> 16.7 us  [the longest x2 8.62 us: attend(): pl.pallas_call(functools.partial(attend_kernel, near=near, shard_rows=sha...]
  transfers between devices with their start and end apart: 2 -> 6, of which waited for: 1 -> 4; matrix products, arithmetic and copies ran while one was open for 0% -> 0% of each run, Pallas kernels for 4% -> 6%
where the time goes in v3:
time: 111 us
  blocking collectives  59.3 us (53%)
  starting transfers between devices  20.9 us (19%)
  Pallas kernels  16.7 us (15%)
  waiting for transfers between devices  12.6 us (11%)
    all_to_all x1, blocking collectives, local(): lax.all_to_all(shard_data, 'seq', split_axis=0, concat_axis=0, tiled=True)  59.3 us
    pallas_call x2, Pallas kernels, attend(): pl.pallas_call(functools.partial(attend_kernel, near=near, shard_rows=sha...  8.62 us
    ppermute x3, starting transfers between devices, local(): lax.ppermute(near[m], 'seq', [(i, i ^ m) for i in range(device_count)])  7.87 us
    ppermute x3, waiting for transfers between devices, local(): lax.ppermute(near[m], 'seq', [(i, i ^ m) for i in range(device_count)])  7.83 us
    ppermute x1, starting transfers between devices, local(): from_across = lax.ppermute(inter, 'seq', across)  5.39 us
    pallas_call x1, Pallas kernels, select_rows(): pl.pallas_call(functools.partial(select_kernel, groups=groups, parts=part...  4.52 us
    ppermute x1, starting transfers between devices, local(): from_within = lax.ppermute(intra, 'seq', within)  4.12 us
    all_to_all x1, starting transfers between devices, local(): far = lax.all_to_all(far, 'seq', split_axis=0, concat_axis=0, tiled=True)  3.5 us
  transfers between devices with their start and end apart: 6, of which 4 were waited for; matrix products, arithmetic and copies ran while one was open for 0% of the time, Pallas kernels for 6%

profile of v3, /device:TPU:1, one launch (start us, length us, event | category | flops | bytes accessed | tf_op | source)
XLA Modules:
  0.0 110.8 jit_solution(8599059431009843756)
XLA Ops:
  0.0 0.0 copy-start
  0.0 0.7 copy-done
  0.7 2.6 %shard_map.29 = bf16[16,80,384]{2,1,0:T(8,128)(2,1)S(1)} custom-call(s32[2560]{0:T(1024)S(1)} %copy-done, bf16[320,6144]{1,0:T(8,128)(2,1)} %tile_ref.1), custom_call_target="tpu_custom_call" | custom-call | tf_op jit(solution)/shard_map/pallas_call | solution.py:52
  3.3 5.4 %collective-permute-start = (bf16[16,80,384]{2,1,0:T(8,128)(2,1)S(1)}, bf16[16,80,384]{2,1,0:T(8,128)(2,1)S(1)}, u32[]{:S(2)}, u32[]{:S(2)}) collective-permute-start(bf16[16,80,384]{2,1,0:T(8,128)(2,1)S(1)} %shard_map.29), channel_id=1, source_target_pairs={{1,2},{2,1},{3,4},{4,3},{5,6},{6,5},{7,8},{8,7},{9,10},{10,9},{11,... | collective-permute-start | bytes 2949128 | tf_op jit(solution)/shard_map/ppermute | solution.py:249
  8.7 4.5 %shard_map.28 = (bf16[16,160,384]{2,1,0:T(8,128)(2,1)S(1)}, bf16[16,80,384]{2,1,0:T(8,128)(2,1)S(1)}) custom-call(s32[2560]{0:T(1024)S(1)} %copy-done, bf16[320,6144]{1,0:T(8,128)(2,1)} %tile_ref.1, bf16[320,6144]{1,0:T(8,128)(2,1)} %tile_ref.1, bf16[320,6144]{1,0:T(8,128)(2,1)} %tile_ref.1), custom_call_target="tpu_custom_call" | custom-call | tf_op jit(solution)/shard_map/pallas_call | solution.py:100
  13.2 4.1 %collective-permute-start.1 = (bf16[16,80,384]{2,1,0:T(8,128)(2,1)S(1)}, bf16[16,80,384]{2,1,0:T(8,128)(2,1)S(1)}, u32[]{:S(2)}, u32[]{:S(2)}) collective-permute-start(bf16[16,80,384]{2,1,0:T(8,128)(2,1)S(1)} %get-tuple-element.12), channel_id=1, source_target_pairs={{0,1},{1,0},{2,3},{3,2},{4,5},{5,4},{6,7},{7,6},{8,9},{9,8},{10,11... | collective-permute-start | bytes 2949128 | tf_op jit(solution)/shard_map/ppermute | solution.py:251
  17.3 3.1 %collective-permute-done = bf16[16,80,384]{2,1,0:T(8,128)(2,1)S(1)} collective-permute-done((bf16[16,80,384]{2,1,0:T(8,128)(2,1)S(1)}, bf16[16,80,384]{2,1,0:T(8,128)(2,1)S(1)}, u32[]{:S(2)}, u32[]{:S(2)}) %collective-permute-start) | collective-permute-done | bytes 983072 | tf_op jit(solution)/shard_map/ppermute | solution.py:249
  20.4 0.0 collective-permute-done.1
  20.4 0.6 maximum_add_fusion
  21.0 59.3 %all_to_all.10 = bf16[16,160,384]{2,1,0:T(8,128)(2,1)S(1)} all-to-all(bf16[16,160,384]{2,1,0:T(8,128)(2,1)S(1)} %maximum_add_fusion), channel_id=1, replica_groups=mesh['dp'=32,'seq'=16] {'seq'}, dimensions={0} | all-to-all | bytes 3932160 | tf_op jit(solution)/shard_map/all_to_all | solution.py:253
  80.3 6.6 %shard_map.30 = bf16[16,160,128]{2,1,0:T(8,128)(2,1)} custom-call(bf16[2560,384]{1,0:T(8,128)(2,1)S(1)} %bitcast.1), custom_call_target="tpu_custom_call" | custom-call | tf_op jit(solution)/shard_map/pallas_call | solution.py:196
  86.9 3.5 %all-to-all-start.1 = ((bf16[16,160,128]{2,1,0:T(8,128)(2,1)}), bf16[16,160,128]{2,1,0:T(8,128)(2,1)S(1)}, u32[]{:S(2)}, u32[]{:S(2)}) async-start(bf16[16,160,128]{2,1,0:T(8,128)(2,1)} %shard_map.30), calls=%async_computation.1 | async-start | bytes 1310720 | tf_op jit(solution)/shard_map/all_to_all | solution.py:256
  90.4 2.1 %shard_map.31 = (bf16[160,128]{1,0:T(8,128)(2,1)S(1)}, bf16[160,128]{1,0:T(8,128)(2,1)S(1)}, bf16[160,128]{1,0:T(8,128)(2,1)S(1)}, bf16[160,128]{1,0:T(8,128)(2,1)S(1)}) custom-call(bf16[2560,384]{1,0:T(8,128)(2,1)S(1)} %bitcast.2), custom_call_target="tpu_custom_call" | custom-call | tf_op jit(solution)/shard_map/pallas_call | solution.py:196
  92.4 1.9 %collective-permute-start.2 = (bf16[160,128]{1,0:T(8,128)(2,1)S(1)}, bf16[160,128]{1,0:T(8,128)(2,1)S(1)}, u32[]{:S(2)}, u32[]{:S(2)}) collective-permute-start(bf16[160,128]{1,0:T(8,128)(2,1)S(1)} %get-tuple-element.14), channel_id=1, source_target_pairs={{0,1},{1,0},{2,3},{3,2},{4,5},{5,4},{6,7},{7,6},{8,9},{9,8},{10,11... | collective-permute-start | bytes 122888 | tf_op jit(solution)/shard_map/ppermute | solution.py:259
  94.4 3.0 %collective-permute-start.3 = (bf16[160,128]{1,0:T(8,128)(2,1)S(1)}, bf16[160,128]{1,0:T(8,128)(2,1)S(1)}, u32[]{:S(2)}, u32[]{:S(2)}) collective-permute-start(bf16[160,128]{1,0:T(8,128)(2,1)S(1)} %get-tuple-element.15), channel_id=1, source_target_pairs={{0,2},{1,3},{2,0},{3,1},{4,6},{5,7},{6,4},{7,5},{8,10},{9,11},{10,... | collective-permute-start | bytes 122888 | tf_op jit(solution)/shard_map/ppermute | solution.py:259
  97.4 2.9 %collective-permute-start.4 = (bf16[160,128]{1,0:T(8,128)(2,1)S(1)}, bf16[160,128]{1,0:T(8,128)(2,1)S(1)}, u32[]{:S(2)}, u32[]{:S(2)}) collective-permute-start(bf16[160,128]{1,0:T(8,128)(2,1)S(1)} %get-tuple-element.16), channel_id=1, source_target_pairs={{0,3},{1,2},{2,1},{3,0},{4,7},{5,6},{6,5},{7,4},{8,11},{9,10},{10,... | collective-permute-start | bytes 122888 | tf_op jit(solution)/shard_map/ppermute | solution.py:259
  100.3 0.0 collective-permute-done.2.refs_1_
  100.3 6.8 %collective-permute-done.3.refs_2_ = bf16[160,128]{1,0:T(8,128)(2,1)S(1)} collective-permute-done((bf16[160,128]{1,0:T(8,128)(2,1)S(1)}, bf16[160,128]{1,0:T(8,128)(2,1)S(1)}, u32[]{:S(2)}, u32[]{:S(2)}) %collective-permute-start.3) | collective-permute-done | bytes 40992 | tf_op jit(solution)/shard_map/ppermute | solution.py:259
  107.1 1.1 collective-permute-done.4.refs_3_
  108.2 1.6 %all-to-all-done.1.far_ref = bf16[16,160,128]{2,1,0:T(8,128)(2,1)S(1)} async-done(((bf16[16,160,128]{2,1,0:T(8,128)(2,1)}), bf16[16,160,128]{2,1,0:T(8,128)(2,1)S(1)}, u32[]{:S(2)}, u32[]{:S(2)}) %all-to-all-start.1) | async-done | bytes 655392 | tf_op jit(solution)/shard_map/all_to_all | solution.py:256
  109.8 1.0 shard_map.32
Async XLA Ops:
  0.0 0.7 copy-start
  3.3 17.2 %collective-permute-start = (bf16[16,80,384]{2,1,0:T(8,128)(2,1)S(1)}, bf16[16,80,384]{2,1,0:T(8,128)(2,1)S(1)}, u32[]{:S(2)}, u32[]{:S(2)}) collective-permute-start(bf16[16,80,384]{2,1,0:T(8,128)(2,1)S(1)} %shard_map.29), channel_id=1, source_target_pairs={{1,2},{2,1},{3,4},{4,3},{5,6},{6,5},{7,8},{8,7},{9,10},{10,9},{11,... | collective-permute-start | bytes 2949128 | tf_op jit(solution)/shard_map/ppermute | solution.py:249
  13.2 7.2 %collective-permute-start.1 = (bf16[16,80,384]{2,1,0:T(8,128)(2,1)S(1)}, bf16[16,80,384]{2,1,0:T(8,128)(2,1)S(1)}, u32[]{:S(2)}, u32[]{:S(2)}) collective-permute-start(bf16[16,80,384]{2,1,0:T(8,128)(2,1)S(1)} %get-tuple-element.12), channel_id=1, source_target_pairs={{0,1},{1,0},{2,3},{3,2},{4,5},{5,4},{6,7},{7,6},{8,9},{9,8},{10,11... | collective-permute-start | bytes 2949128 | tf_op jit(solution)/shard_map/ppermute | solution.py:251
  86.9 22.9 %all-to-all-start.1 = ((bf16[16,160,128]{2,1,0:T(8,128)(2,1)}), bf16[16,160,128]{2,1,0:T(8,128)(2,1)S(1)}, u32[]{:S(2)}, u32[]{:S(2)}) async-start(bf16[16,160,128]{2,1,0:T(8,128)(2,1)} %shard_map.30), calls=%async_computation.1 | async-start | bytes 1310720 | tf_op jit(solution)/shard_map/all_to_all | solution.py:256
  92.4 7.9 %collective-permute-start.2 = (bf16[160,128]{1,0:T(8,128)(2,1)S(1)}, bf16[160,128]{1,0:T(8,128)(2,1)S(1)}, u32[]{:S(2)}, u32[]{:S(2)}) collective-permute-start(bf16[160,128]{1,0:T(8,128)(2,1)S(1)} %get-tuple-element.14), channel_id=1, source_target_pairs={{0,1},{1,0},{2,3},{3,2},{4,5},{5,4},{6,7},{7,6},{8,9},{9,8},{10,11... | collective-permute-start | bytes 122888 | tf_op jit(solution)/shard_map/ppermute | solution.py:259
  94.4 12.7 %collective-permute-start.3 = (bf16[160,128]{1,0:T(8,128)(2,1)S(1)}, bf16[160,128]{1,0:T(8,128)(2,1)S(1)}, u32[]{:S(2)}, u32[]{:S(2)}) collective-permute-start(bf16[160,128]{1,0:T(8,128)(2,1)S(1)} %get-tuple-element.15), channel_id=1, source_target_pairs={{0,2},{1,3},{2,0},{3,1},{4,6},{5,7},{6,4},{7,5},{8,10},{9,11},{10,... | collective-permute-start | bytes 122888 | tf_op jit(solution)/shard_map/ppermute | solution.py:259
  97.4 10.7 %collective-permute-start.4 = (bf16[160,128]{1,0:T(8,128)(2,1)S(1)}, bf16[160,128]{1,0:T(8,128)(2,1)S(1)}, u32[]{:S(2)}, u32[]{:S(2)}) collective-permute-start(bf16[160,128]{1,0:T(8,128)(2,1)S(1)} %get-tuple-element.16), channel_id=1, source_target_pairs={{0,3},{1,2},{2,1},{3,0},{4,7},{5,6},{6,5},{7,4},{8,11},{9,10},{10,... | collective-permute-start | bytes 122888 | tf_op jit(solution)/shard_map/ppermute | solution.py:259

commit v4 on v3

--- a/solution.py
+++ b/solution.py
@@ -10,7 +10,9 @@
 H = 16
 HD = 128
 CORES = 2
-NEAR = 4
+NEAR = 5
+NEAR_BLOCKS = (3, 2)
+FAR_BLOCKS = (3, 3, 3, 2)
 LOG2E = 1.4426950408889634
 VMEM_BYTES = 50 * 1024 * 1024
 
@@ -121,7 +123,6 @@
     value_rows = jnp.concatenate([triple_ref[:, 2 * HD :], ones], axis=1)
     scale = HD ** (-0.5) * LOG2E
     half = shard_rows // 2
-    block = 2 * shard_rows
     device = lax.axis_index("seq")
     count = queries_ref.shape[0] // shard_rows
 
@@ -136,9 +137,12 @@
             start = i * shard_rows + j * half
             queries_ref[start : start + half, :] = triple_ref[pl.ds(rows, half), :HD]
 
-    def scores_of(start):
+    sizes = [size * shard_rows for size in (NEAR_BLOCKS if near else FAR_BLOCKS)]
+    bounds = [(sum(sizes[:i]), sum(sizes[: i + 1])) for i in range(len(sizes))]
+
+    def scores_of(start, stop):
         return lax.dot_general(
-            queries_ref[start : start + block, :],
+            queries_ref[start:stop, :],
             key_rows,
             (((1,), (1,)), ((), ())),
             preferred_element_type=jnp.float32,
@@ -159,27 +163,25 @@
         for i in range(NEAR):
             send(zeros_ref, device ^ i)
 
-    def write(start, weights):
+    def write(start, stop, weights):
         mixed = jnp.dot(weights, value_rows, preferred_element_type=jnp.float32)
         result = mixed[:, :HD] / mixed[:, HD:]
-        result_ref[start : start + block, :] = result.astype(result_ref.dtype)
-        for at in range(start, start + block, shard_rows):
+        result_ref[start:stop, :] = result.astype(result_ref.dtype)
+        for at in range(start, stop, shard_rows):
             if near:
                 out_refs[at // shard_rows][...] = result_ref[at : at + shard_rows, :]
             else:
                 send(result_ref.at[at : at + shard_rows, :], shard_of(at // shard_rows))
 
-    starts = range(0, count * shard_rows, block)
-    scores = scores_of(0)
+    scores = scores_of(*bounds[0])
     weights = None
-    for start in starts:
-        later = scores_of(start + block) if start + block < starts.stop else None
+    for i in range(len(bounds)):
+        later = scores_of(*bounds[i + 1]) if i + 1 < len(bounds) else None
         newer = weights_of(scores)
         if weights is not None:
-            write(start - block, weights)
+            write(*bounds[i - 1], weights)
         scores, weights = later, newer
-    write(starts[-1], weights)
-
+    write(*bounds[-1], weights)
     for copy in copies:
         copy.wait()
 

time: 111 us -> 111 us (level)
  waiting for transfers between devices: 12.6 us -> 8.41 us
  starting transfers between devices: 20.9 us -> 24.5 us
    ppermute x3 -> x4, starting transfers between devices: 7.87 us -> 11.5 us  [local(): lax.ppermute(near[m], 'seq', [(i, i ^ m) for i in range(device_count)])]
    ppermute x3 -> x4, waiting for transfers between devices: 7.83 us -> 4.54 us  [local(): lax.ppermute(near[m], 'seq', [(i, i ^ m) for i in range(device_count)])]
  transfers between devices with their start and end apart: 6 -> 7, of which waited for: 4 -> 4; matrix products, arithmetic and copies ran while one was open for 0% -> 0% of each run, Pallas kernels for 6% -> 6%
where the time goes in v4:
time: 111 us; the launch traced here: 110 us
  blocking collectives  59.3 us (53%)
  starting transfers between devices  24.5 us (22%)
  Pallas kernels  16.8 us (15%)
  waiting for transfers between devices  8.41 us (8%)
    all_to_all x1, blocking collectives, local(): lax.all_to_all(shard_data, 'seq', split_axis=0, concat_axis=0, tiled=True)  59.3 us
    ppermute x4, starting transfers between devices, local(): lax.ppermute(near[m], 'seq', [(i, i ^ m) for i in range(device_count)])  11.5 us
    pallas_call x2, Pallas kernels, attend(): pl.pallas_call(functools.partial(attend_kernel, near=near, shard_rows=sha...  8.77 us
    ppermute x1, starting transfers between devices, local(): from_across = lax.ppermute(inter, 'seq', across)  5.39 us
    ppermute x4, waiting for transfers between devices, local(): lax.ppermute(near[m], 'seq', [(i, i ^ m) for i in range(device_count)])  4.54 us
    pallas_call x1, Pallas kernels, select_rows(): pl.pallas_call(functools.partial(select_kernel, groups=groups, parts=part...  4.52 us
    ppermute x1, starting transfers between devices, local(): from_within = lax.ppermute(intra, 'seq', within)  4.12 us
    all_to_all x1, starting transfers between devices, local(): far = lax.all_to_all(far, 'seq', split_axis=0, concat_axis=0, tiled=True)  3.5 us
  transfers between devices with their start and end apart: 7, of which 4 were waited for; matrix products, arithmetic and copies ran while one was open for 0% of the time, Pallas kernels for 6%

profile of v4, /device:TPU:1, one launch (start us, length us, event | category | flops | bytes accessed | tf_op | source)
XLA Modules:
  0.0 110.4 jit_solution(15428345815510716450)
XLA Ops:
  0.0 0.0 copy-start
  0.0 0.7 copy-done
  0.7 2.6 %shard_map.29 = bf16[16,80,384]{2,1,0:T(8,128)(2,1)S(1)} custom-call(s32[2560]{0:T(1024)S(1)} %copy-done, bf16[320,6144]{1,0:T(8,128)(2,1)} %tile_ref.1), custom_call_target="tpu_custom_call" | custom-call | tf_op jit(solution)/shard_map/pallas_call | solution.py:54
  3.3 5.4 %collective-permute-start = (bf16[16,80,384]{2,1,0:T(8,128)(2,1)S(1)}, bf16[16,80,384]{2,1,0:T(8,128)(2,1)S(1)}, u32[]{:S(2)}, u32[]{:S(2)}) collective-permute-start(bf16[16,80,384]{2,1,0:T(8,128)(2,1)S(1)} %shard_map.29), channel_id=1, source_target_pairs={{1,2},{2,1},{3,4},{4,3},{5,6},{6,5},{7,8},{8,7},{9,10},{10,9},{11,... | collective-permute-start | bytes 2949128 | tf_op jit(solution)/shard_map/ppermute | solution.py:251
  8.7 4.5 %shard_map.28 = (bf16[16,160,384]{2,1,0:T(8,128)(2,1)S(1)}, bf16[16,80,384]{2,1,0:T(8,128)(2,1)S(1)}) custom-call(s32[2560]{0:T(1024)S(1)} %copy-done, bf16[320,6144]{1,0:T(8,128)(2,1)} %tile_ref.1, bf16[320,6144]{1,0:T(8,128)(2,1)} %tile_ref.1, bf16[320,6144]{1,0:T(8,128)(2,1)} %tile_ref.1), custom_call_target="tpu_custom_call" | custom-call | tf_op jit(solution)/shard_map/pallas_call | solution.py:102
  13.2 4.1 %collective-permute-start.1 = (bf16[16,80,384]{2,1,0:T(8,128)(2,1)S(1)}, bf16[16,80,384]{2,1,0:T(8,128)(2,1)S(1)}, u32[]{:S(2)}, u32[]{:S(2)}) collective-permute-start(bf16[16,80,384]{2,1,0:T(8,128)(2,1)S(1)} %get-tuple-element.13), channel_id=1, source_target_pairs={{0,1},{1,0},{2,3},{3,2},{4,5},{5,4},{6,7},{7,6},{8,9},{9,8},{10,11... | collective-permute-start | bytes 2949128 | tf_op jit(solution)/shard_map/ppermute | solution.py:253
  17.3 3.1 %collective-permute-done = bf16[16,80,384]{2,1,0:T(8,128)(2,1)S(1)} collective-permute-done((bf16[16,80,384]{2,1,0:T(8,128)(2,1)S(1)}, bf16[16,80,384]{2,1,0:T(8,128)(2,1)S(1)}, u32[]{:S(2)}, u32[]{:S(2)}) %collective-permute-start) | collective-permute-done | bytes 983072 | tf_op jit(solution)/shard_map/ppermute | solution.py:251
  20.4 0.0 collective-permute-done.1
  20.4 0.6 maximum_add_fusion
  21.0 59.3 %all_to_all.10 = bf16[16,160,384]{2,1,0:T(8,128)(2,1)S(1)} all-to-all(bf16[16,160,384]{2,1,0:T(8,128)(2,1)S(1)} %maximum_add_fusion), channel_id=1, replica_groups=mesh['dp'=32,'seq'=16] {'seq'}, dimensions={0} | all-to-all | bytes 3932160 | tf_op jit(solution)/shard_map/all_to_all | solution.py:255
  80.3 6.2 %shard_map.30 = bf16[16,160,128]{2,1,0:T(8,128)(2,1)} custom-call(bf16[2560,384]{1,0:T(8,128)(2,1)S(1)} %bitcast.1), custom_call_target="tpu_custom_call" | custom-call | tf_op jit(solution)/shard_map/pallas_call | solution.py:198
  86.5 3.5 %all-to-all-start.1 = ((bf16[16,160,128]{2,1,0:T(8,128)(2,1)}), bf16[16,160,128]{2,1,0:T(8,128)(2,1)S(1)}, u32[]{:S(2)}, u32[]{:S(2)}) async-start(bf16[16,160,128]{2,1,0:T(8,128)(2,1)} %shard_map.30), calls=%async_computation.1 | async-start | bytes 1310720 | tf_op jit(solution)/shard_map/all_to_all | solution.py:258
  90.0 2.6 %shard_map.31 = (bf16[160,128]{1,0:T(8,128)(2,1)S(1)}, bf16[160,128]{1,0:T(8,128)(2,1)S(1)}, bf16[160,128]{1,0:T(8,128)(2,1)S(1)}, bf16[160,128]{1,0:T(8,128)(2,1)S(1)}, bf16[160,128]{1,0:T(8,128)(2,1)S(1)}) custom-call(bf16[2560,384]{1,0:T(8,128)(2,1)S(1)} %bitcast.2), custom_call_target="tpu_custom_call" | custom-call | tf_op jit(solution)/shard_map/pallas_call | solution.py:198
  92.6 1.9 %collective-permute-start.2 = (bf16[160,128]{1,0:T(8,128)(2,1)S(1)}, bf16[160,128]{1,0:T(8,128)(2,1)S(1)}, u32[]{:S(2)}, u32[]{:S(2)}) collective-permute-start(bf16[160,128]{1,0:T(8,128)(2,1)S(1)} %get-tuple-element.15), channel_id=1, source_target_pairs={{0,1},{1,0},{2,3},{3,2},{4,5},{5,4},{6,7},{7,6},{8,9},{9,8},{10,11... | collective-permute-start | bytes 122888 | tf_op jit(solution)/shard_map/ppermute | solution.py:261
  94.5 3.0 %collective-permute-start.3 = (bf16[160,128]{1,0:T(8,128)(2,1)S(1)}, bf16[160,128]{1,0:T(8,128)(2,1)S(1)}, u32[]{:S(2)}, u32[]{:S(2)}) collective-permute-start(bf16[160,128]{1,0:T(8,128)(2,1)S(1)} %get-tuple-element.16), channel_id=1, source_target_pairs={{0,2},{1,3},{2,0},{3,1},{4,6},{5,7},{6,4},{7,5},{8,10},{9,11},{10,... | collective-permute-start | bytes 122888 | tf_op jit(solution)/shard_map/ppermute | solution.py:261
  97.6 2.9 %collective-permute-start.4 = (bf16[160,128]{1,0:T(8,128)(2,1)S(1)}, bf16[160,128]{1,0:T(8,128)(2,1)S(1)}, u32[]{:S(2)}, u32[]{:S(2)}) collective-permute-start(bf16[160,128]{1,0:T(8,128)(2,1)S(1)} %get-tuple-element.17), channel_id=1, source_target_pairs={{0,3},{1,2},{2,1},{3,0},{4,7},{5,6},{6,5},{7,4},{8,11},{9,10},{10,... | collective-permute-start | bytes 122888 | tf_op jit(solution)/shard_map/ppermute | solution.py:261
  100.5 3.6 %collective-permute-start.5 = (bf16[160,128]{1,0:T(8,128)(2,1)S(1)}, bf16[160,128]{1,0:T(8,128)(2,1)S(1)}, u32[]{:S(2)}, u32[]{:S(2)}) collective-permute-start(bf16[160,128]{1,0:T(8,128)(2,1)S(1)} %get-tuple-element.18), channel_id=1, source_target_pairs={{0,4},{1,5},{2,6},{3,7},{4,0},{5,1},{6,2},{7,3},{8,12},{9,13},{10,... | collective-permute-start | bytes 122888 | tf_op jit(solution)/shard_map/ppermute | solution.py:261
  104.1 0.0 collective-permute-done.2.refs_1_
  104.1 2.8 %collective-permute-done.3.refs_2_ = bf16[160,128]{1,0:T(8,128)(2,1)S(1)} collective-permute-done((bf16[160,128]{1,0:T(8,128)(2,1)S(1)}, bf16[160,128]{1,0:T(8,128)(2,1)S(1)}, u32[]{:S(2)}, u32[]{:S(2)}) %collective-permute-start.3) | collective-permute-done | bytes 40992 | tf_op jit(solution)/shard_map/ppermute | solution.py:261
  106.9 1.7 %collective-permute-done.4.refs_3_ = bf16[160,128]{1,0:T(8,128)(2,1)S(1)} collective-permute-done((bf16[160,128]{1,0:T(8,128)(2,1)S(1)}, bf16[160,128]{1,0:T(8,128)(2,1)S(1)}, u32[]{:S(2)}, u32[]{:S(2)}) %collective-permute-start.4) | collective-permute-done | bytes 40992 | tf_op jit(solution)/shard_map/ppermute | solution.py:261
  108.6 0.0 collective-permute-done.5.refs_4_
  108.6 0.8 all-to-all-done.1.far_ref
  109.4 1.0 shard_map.32
Async XLA Ops:
  0.0 0.7 copy-start
  3.3 17.2 %collective-permute-start = (bf16[16,80,384]{2,1,0:T(8,128)(2,1)S(1)}, bf16[16,80,384]{2,1,0:T(8,128)(2,1)S(1)}, u32[]{:S(2)}, u32[]{:S(2)}) collective-permute-start(bf16[16,80,384]{2,1,0:T(8,128)(2,1)S(1)} %shard_map.29), channel_id=1, source_target_pairs={{1,2},{2,1},{3,4},{4,3},{5,6},{6,5},{7,8},{8,7},{9,10},{10,9},{11,... | collective-permute-start | bytes 2949128 | tf_op jit(solution)/shard_map/ppermute | solution.py:251
  13.2 7.2 %collective-permute-start.1 = (bf16[16,80,384]{2,1,0:T(8,128)(2,1)S(1)}, bf16[16,80,384]{2,1,0:T(8,128)(2,1)S(1)}, u32[]{:S(2)}, u32[]{:S(2)}) collective-permute-start(bf16[16,80,384]{2,1,0:T(8,128)(2,1)S(1)} %get-tuple-element.13), channel_id=1, source_target_pairs={{0,1},{1,0},{2,3},{3,2},{4,5},{5,4},{6,7},{7,6},{8,9},{9,8},{10,11... | collective-permute-start | bytes 2949128 | tf_op jit(solution)/shard_map/ppermute | solution.py:253
  86.5 22.9 %all-to-all-start.1 = ((bf16[16,160,128]{2,1,0:T(8,128)(2,1)}), bf16[16,160,128]{2,1,0:T(8,128)(2,1)S(1)}, u32[]{:S(2)}, u32[]{:S(2)}) async-start(bf16[16,160,128]{2,1,0:T(8,128)(2,1)} %shard_map.30), calls=%async_computation.1 | async-start | bytes 1310720 | tf_op jit(solution)/shard_map/all_to_all | solution.py:258
  92.6 11.5 %collective-permute-start.2 = (bf16[160,128]{1,0:T(8,128)(2,1)S(1)}, bf16[160,128]{1,0:T(8,128)(2,1)S(1)}, u32[]{:S(2)}, u32[]{:S(2)}) collective-permute-start(bf16[160,128]{1,0:T(8,128)(2,1)S(1)} %get-tuple-element.15), channel_id=1, source_target_pairs={{0,1},{1,0},{2,3},{3,2},{4,5},{5,4},{6,7},{7,6},{8,9},{9,8},{10,11... | collective-permute-start | bytes 122888 | tf_op jit(solution)/shard_map/ppermute | solution.py:261
  94.5 12.4 %collective-permute-start.3 = (bf16[160,128]{1,0:T(8,128)(2,1)S(1)}, bf16[160,128]{1,0:T(8,128)(2,1)S(1)}, u32[]{:S(2)}, u32[]{:S(2)}) collective-permute-start(bf16[160,128]{1,0:T(8,128)(2,1)S(1)} %get-tuple-element.16), channel_id=1, source_target_pairs={{0,2},{1,3},{2,0},{3,1},{4,6},{5,7},{6,4},{7,5},{8,10},{9,11},{10,... | collective-permute-start | bytes 122888 | tf_op jit(solution)/shard_map/ppermute | solution.py:261
  97.6 11.1 %collective-permute-start.4 = (bf16[160,128]{1,0:T(8,128)(2,1)S(1)}, bf16[160,128]{1,0:T(8,128)(2,1)S(1)}, u32[]{:S(2)}, u32[]{:S(2)}) collective-permute-start(bf16[160,128]{1,0:T(8,128)(2,1)S(1)} %get-tuple-element.17), channel_id=1, source_target_pairs={{0,3},{1,2},{2,1},{3,0},{4,7},{5,6},{6,5},{7,4},{8,11},{9,10},{10,... | collective-permute-start | bytes 122888 | tf_op jit(solution)/shard_map/ppermute | solution.py:261
  100.5 8.2 %collective-permute-start.5 = (bf16[160,128]{1,0:T(8,128)(2,1)S(1)}, bf16[160,128]{1,0:T(8,128)(2,1)S(1)}, u32[]{:S(2)}, u32[]{:S(2)}) collective-permute-start(bf16[160,128]{1,0:T(8,128)(2,1)S(1)} %get-tuple-element.18), channel_id=1, source_target_pairs={{0,4},{1,5},{2,6},{3,7},{4,0},{5,1},{6,2},{7,3},{8,12},{9,13},{10,... | collective-permute-start | bytes 122888 | tf_op jit(solution)/shard_map/ppermute | solution.py:261

commit v5 on v4

--- a/solution.py
+++ b/solution.py
@@ -10,9 +10,9 @@
 H = 16
 HD = 128
 CORES = 2
-NEAR = 5
-NEAR_BLOCKS = (3, 2)
-FAR_BLOCKS = (3, 3, 3, 2)
+NEAR = 4
+NEAR_BLOCKS = (2, 2)
+FAR_BLOCKS = (3, 3, 3, 3)
 LOG2E = 1.4426950408889634
 VMEM_BYTES = 50 * 1024 * 1024
 

time: 111 us -> 111 us (level)
  waiting for transfers between devices: 8.41 us -> 12.6 us
  starting transfers between devices: 24.5 us -> 20.9 us
    ppermute x4 -> x3, starting transfers between devices: 11.5 us -> 7.87 us  [local(): lax.ppermute(near[m], 'seq', [(i, i ^ m) for i in range(device_count)])]
    ppermute x4 -> x3, waiting for transfers between devices: 4.54 us -> 7.82 us  [local(): lax.ppermute(near[m], 'seq', [(i, i ^ m) for i in range(device_count)])]
  transfers between devices with their start and end apart: 7 -> 6, of which waited for: 4 -> 4; matrix products, arithmetic and copies ran while one was open for 0% -> 0% of each run, Pallas kernels for 6% -> 6%
where the time goes in v5:
time: 111 us
  blocking collectives  59.3 us (53%)
  starting transfers between devices  20.9 us (19%)
  Pallas kernels  16.6 us (15%)
  waiting for transfers between devices  12.6 us (11%)
    all_to_all x1, blocking collectives, local(): lax.all_to_all(shard_data, 'seq', split_axis=0, concat_axis=0, tiled=True)  59.3 us
    pallas_call x2, Pallas kernels, attend(): pl.pallas_call(functools.partial(attend_kernel, near=near, shard_rows=sha...  8.58 us
    ppermute x3, starting transfers between devices, local(): lax.ppermute(near[m], 'seq', [(i, i ^ m) for i in range(device_count)])  7.87 us
    ppermute x3, waiting for transfers between devices, local(): lax.ppermute(near[m], 'seq', [(i, i ^ m) for i in range(device_count)])  7.82 us
    ppermute x1, starting transfers between devices, local(): from_across = lax.ppermute(inter, 'seq', across)  5.39 us
    pallas_call x1, Pallas kernels, select_rows(): pl.pallas_call(functools.partial(select_kernel, groups=groups, parts=part...  4.52 us
    ppermute x1, starting transfers between devices, local(): from_within = lax.ppermute(intra, 'seq', within)  4.12 us
    all_to_all x1, starting transfers between devices, local(): far = lax.all_to_all(far, 'seq', split_axis=0, concat_axis=0, tiled=True)  3.5 us
  transfers between devices with their start and end apart: 6, of which 4 were waited for; matrix products, arithmetic and copies ran while one was open for 0% of the time, Pallas kernels for 6%

profile of v5, /device:TPU:1, one launch (start us, length us, event | category | flops | bytes accessed | tf_op | source)
XLA Modules:
  0.0 110.7 jit_solution(5600190219825772130)
XLA Ops:
  0.0 0.0 copy-start
  0.0 0.7 copy-done
  0.7 2.6 %shard_map.29 = bf16[16,80,384]{2,1,0:T(8,128)(2,1)S(1)} custom-call(s32[2560]{0:T(1024)S(1)} %copy-done, bf16[320,6144]{1,0:T(8,128)(2,1)} %tile_ref.1), custom_call_target="tpu_custom_call" | custom-call | tf_op jit(solution)/shard_map/pallas_call | solution.py:54
  3.3 5.4 %collective-permute-start = (bf16[16,80,384]{2,1,0:T(8,128)(2,1)S(1)}, bf16[16,80,384]{2,1,0:T(8,128)(2,1)S(1)}, u32[]{:S(2)}, u32[]{:S(2)}) collective-permute-start(bf16[16,80,384]{2,1,0:T(8,128)(2,1)S(1)} %shard_map.29), channel_id=1, source_target_pairs={{1,2},{2,1},{3,4},{4,3},{5,6},{6,5},{7,8},{8,7},{9,10},{10,9},{11,... | collective-permute-start | bytes 2949128 | tf_op jit(solution)/shard_map/ppermute | solution.py:251
  8.7 4.5 %shard_map.28 = (bf16[16,160,384]{2,1,0:T(8,128)(2,1)S(1)}, bf16[16,80,384]{2,1,0:T(8,128)(2,1)S(1)}) custom-call(s32[2560]{0:T(1024)S(1)} %copy-done, bf16[320,6144]{1,0:T(8,128)(2,1)} %tile_ref.1, bf16[320,6144]{1,0:T(8,128)(2,1)} %tile_ref.1, bf16[320,6144]{1,0:T(8,128)(2,1)} %tile_ref.1), custom_call_target="tpu_custom_call" | custom-call | tf_op jit(solution)/shard_map/pallas_call | solution.py:102
  13.2 4.1 %collective-permute-start.1 = (bf16[16,80,384]{2,1,0:T(8,128)(2,1)S(1)}, bf16[16,80,384]{2,1,0:T(8,128)(2,1)S(1)}, u32[]{:S(2)}, u32[]{:S(2)}) collective-permute-start(bf16[16,80,384]{2,1,0:T(8,128)(2,1)S(1)} %get-tuple-element.12), channel_id=1, source_target_pairs={{0,1},{1,0},{2,3},{3,2},{4,5},{5,4},{6,7},{7,6},{8,9},{9,8},{10,11... | collective-permute-start | bytes 2949128 | tf_op jit(solution)/shard_map/ppermute | solution.py:253
  17.3 3.1 %collective-permute-done = bf16[16,80,384]{2,1,0:T(8,128)(2,1)S(1)} collective-permute-done((bf16[16,80,384]{2,1,0:T(8,128)(2,1)S(1)}, bf16[16,80,384]{2,1,0:T(8,128)(2,1)S(1)}, u32[]{:S(2)}, u32[]{:S(2)}) %collective-permute-start) | collective-permute-done | bytes 983072 | tf_op jit(solution)/shard_map/ppermute | solution.py:251
  20.4 0.0 collective-permute-done.1
  20.4 0.6 maximum_add_fusion
  21.0 59.3 %all_to_all.10 = bf16[16,160,384]{2,1,0:T(8,128)(2,1)S(1)} all-to-all(bf16[16,160,384]{2,1,0:T(8,128)(2,1)S(1)} %maximum_add_fusion), channel_id=1, replica_groups=mesh['dp'=32,'seq'=16] {'seq'}, dimensions={0} | all-to-all | bytes 3932160 | tf_op jit(solution)/shard_map/all_to_all | solution.py:255
  80.3 6.5 %shard_map.30 = bf16[16,160,128]{2,1,0:T(8,128)(2,1)} custom-call(bf16[2560,384]{1,0:T(8,128)(2,1)S(1)} %bitcast.1), custom_call_target="tpu_custom_call" | custom-call | tf_op jit(solution)/shard_map/pallas_call | solution.py:198
  86.8 3.5 %all-to-all-start.1 = ((bf16[16,160,128]{2,1,0:T(8,128)(2,1)}), bf16[16,160,128]{2,1,0:T(8,128)(2,1)S(1)}, u32[]{:S(2)}, u32[]{:S(2)}) async-start(bf16[16,160,128]{2,1,0:T(8,128)(2,1)} %shard_map.30), calls=%async_computation.1 | async-start | bytes 1310720 | tf_op jit(solution)/shard_map/all_to_all | solution.py:258
  90.3 2.1 %shard_map.31 = (bf16[160,128]{1,0:T(8,128)(2,1)S(1)}, bf16[160,128]{1,0:T(8,128)(2,1)S(1)}, bf16[160,128]{1,0:T(8,128)(2,1)S(1)}, bf16[160,128]{1,0:T(8,128)(2,1)S(1)}) custom-call(bf16[2560,384]{1,0:T(8,128)(2,1)S(1)} %bitcast.2), custom_call_target="tpu_custom_call" | custom-call | tf_op jit(solution)/shard_map/pallas_call | solution.py:198
  92.4 1.9 %collective-permute-start.2 = (bf16[160,128]{1,0:T(8,128)(2,1)S(1)}, bf16[160,128]{1,0:T(8,128)(2,1)S(1)}, u32[]{:S(2)}, u32[]{:S(2)}) collective-permute-start(bf16[160,128]{1,0:T(8,128)(2,1)S(1)} %get-tuple-element.14), channel_id=1, source_target_pairs={{0,1},{1,0},{2,3},{3,2},{4,5},{5,4},{6,7},{7,6},{8,9},{9,8},{10,11... | collective-permute-start | bytes 122888 | tf_op jit(solution)/shard_map/ppermute | solution.py:261
  94.3 3.0 %collective-permute-start.3 = (bf16[160,128]{1,0:T(8,128)(2,1)S(1)}, bf16[160,128]{1,0:T(8,128)(2,1)S(1)}, u32[]{:S(2)}, u32[]{:S(2)}) collective-permute-start(bf16[160,128]{1,0:T(8,128)(2,1)S(1)} %get-tuple-element.15), channel_id=1, source_target_pairs={{0,2},{1,3},{2,0},{3,1},{4,6},{5,7},{6,4},{7,5},{8,10},{9,11},{10,... | collective-permute-start | bytes 122888 | tf_op jit(solution)/shard_map/ppermute | solution.py:261
  97.4 2.9 %collective-permute-start.4 = (bf16[160,128]{1,0:T(8,128)(2,1)S(1)}, bf16[160,128]{1,0:T(8,128)(2,1)S(1)}, u32[]{:S(2)}, u32[]{:S(2)}) collective-permute-start(bf16[160,128]{1,0:T(8,128)(2,1)S(1)} %get-tuple-element.16), channel_id=1, source_target_pairs={{0,3},{1,2},{2,1},{3,0},{4,7},{5,6},{6,5},{7,4},{8,11},{9,10},{10,... | collective-permute-start | bytes 122888 | tf_op jit(solution)/shard_map/ppermute | solution.py:261
  100.3 0.0 collective-permute-done.2.refs_1_
  100.3 6.8 %collective-permute-done.3.refs_2_ = bf16[160,128]{1,0:T(8,128)(2,1)S(1)} collective-permute-done((bf16[160,128]{1,0:T(8,128)(2,1)S(1)}, bf16[160,128]{1,0:T(8,128)(2,1)S(1)}, u32[]{:S(2)}, u32[]{:S(2)}) %collective-permute-start.3) | collective-permute-done | bytes 40992 | tf_op jit(solution)/shard_map/ppermute | solution.py:261
  107.0 1.1 collective-permute-done.4.refs_3_
  108.1 1.6 %all-to-all-done.1.far_ref = bf16[16,160,128]{2,1,0:T(8,128)(2,1)S(1)} async-done(((bf16[16,160,128]{2,1,0:T(8,128)(2,1)}), bf16[16,160,128]{2,1,0:T(8,128)(2,1)S(1)}, u32[]{:S(2)}, u32[]{:S(2)}) %all-to-all-start.1) | async-done | bytes 655392 | tf_op jit(solution)/shard_map/all_to_all | solution.py:258
  109.7 1.0 shard_map.32
Async XLA Ops:
  0.0 0.7 copy-start
  3.3 17.2 %collective-permute-start = (bf16[16,80,384]{2,1,0:T(8,128)(2,1)S(1)}, bf16[16,80,384]{2,1,0:T(8,128)(2,1)S(1)}, u32[]{:S(2)}, u32[]{:S(2)}) collective-permute-start(bf16[16,80,384]{2,1,0:T(8,128)(2,1)S(1)} %shard_map.29), channel_id=1, source_target_pairs={{1,2},{2,1},{3,4},{4,3},{5,6},{6,5},{7,8},{8,7},{9,10},{10,9},{11,... | collective-permute-start | bytes 2949128 | tf_op jit(solution)/shard_map/ppermute | solution.py:251
  13.2 7.2 %collective-permute-start.1 = (bf16[16,80,384]{2,1,0:T(8,128)(2,1)S(1)}, bf16[16,80,384]{2,1,0:T(8,128)(2,1)S(1)}, u32[]{:S(2)}, u32[]{:S(2)}) collective-permute-start(bf16[16,80,384]{2,1,0:T(8,128)(2,1)S(1)} %get-tuple-element.12), channel_id=1, source_target_pairs={{0,1},{1,0},{2,3},{3,2},{4,5},{5,4},{6,7},{7,6},{8,9},{9,8},{10,11... | collective-permute-start | bytes 2949128 | tf_op jit(solution)/shard_map/ppermute | solution.py:253
  86.8 22.9 %all-to-all-start.1 = ((bf16[16,160,128]{2,1,0:T(8,128)(2,1)}), bf16[16,160,128]{2,1,0:T(8,128)(2,1)S(1)}, u32[]{:S(2)}, u32[]{:S(2)}) async-start(bf16[16,160,128]{2,1,0:T(8,128)(2,1)} %shard_map.30), calls=%async_computation.1 | async-start | bytes 1310720 | tf_op jit(solution)/shard_map/all_to_all | solution.py:258
  92.4 7.9 %collective-permute-start.2 = (bf16[160,128]{1,0:T(8,128)(2,1)S(1)}, bf16[160,128]{1,0:T(8,128)(2,1)S(1)}, u32[]{:S(2)}, u32[]{:S(2)}) collective-permute-start(bf16[160,128]{1,0:T(8,128)(2,1)S(1)} %get-tuple-element.14), channel_id=1, source_target_pairs={{0,1},{1,0},{2,3},{3,2},{4,5},{5,4},{6,7},{7,6},{8,9},{9,8},{10,11... | collective-permute-start | bytes 122888 | tf_op jit(solution)/shard_map/ppermute | solution.py:261
  94.3 12.7 %collective-permute-start.3 = (bf16[160,128]{1,0:T(8,128)(2,1)S(1)}, bf16[160,128]{1,0:T(8,128)(2,1)S(1)}, u32[]{:S(2)}, u32[]{:S(2)}) collective-permute-start(bf16[160,128]{1,0:T(8,128)(2,1)S(1)} %get-tuple-element.15), channel_id=1, source_target_pairs={{0,2},{1,3},{2,0},{3,1},{4,6},{5,7},{6,4},{7,5},{8,10},{9,11},{10,... | collective-permute-start | bytes 122888 | tf_op jit(solution)/shard_map/ppermute | solution.py:261
  97.4 10.7 %collective-permute-start.4 = (bf16[160,128]{1,0:T(8,128)(2,1)S(1)}, bf16[160,128]{1,0:T(8,128)(2,1)S(1)}, u32[]{:S(2)}, u32[]{:S(2)}) collective-permute-start(bf16[160,128]{1,0:T(8,128)(2,1)S(1)} %get-tuple-element.16), channel_id=1, source_target_pairs={{0,3},{1,2},{2,1},{3,0},{4,7},{5,6},{6,5},{7,4},{8,11},{9,10},{10,... | collective-permute-start | bytes 122888 | tf_op jit(solution)/shard_map/ppermute | solution.py:261
